TPU v7x, 32 devices: a whole 2x2x4 slice. The times are simulated.
32 devices in a mesh: dp: 8 (over z, y), mp: 4 (over x, core).
Axes of the slice: x: 2, y: 2, z: 4, core: 2. Of those that a mesh axis runs over, the one named last changes fastest.
Arguments:
- hidden_rows: bfloat16 [16384, 768], P(('dp', 'mp')), may hold values from -6 to 6
- token_table: bfloat16 [4096, 768], replicated, may hold values from -6 to 6
- masked_positions: int32 [128, 32], P(('dp', 'mp')), may hold values from 0 to 127, as said below
- masked_counts: int32 [128], P(('dp', 'mp')), may hold values from 6 to 32, as said below
- replace_rows: int32 [128, 32], P(('dp', 'mp')), may hold values from 0 to 4095
- masked_cotangent: bfloat16 [128, 32, 768], P(('dp', 'mp')), may hold values from -6 to 6
- step_number: int32 [1], replicated, may hold values from 2 to 20
- attend_master: float32 [768, 2304], P('dp', 'mp'), may hold values from -0.21875 to 0.21875
- merge_master: float32 [768, 768], P('dp', 'mp'), may hold values from -0.625 to 0.625
- norms_master: float32 [4, 768], P('mp', 'dp'), may hold values from 0.5 to 1.5
- gate_master: float32 [768, 3072], P('dp', 'mp'), may hold values from -0.21875 to 0.21875
- value_master: float32 [768, 3072], P('dp', 'mp'), may hold values from -0.21875 to 0.21875
- down_master: float32 [3072, 768], P('mp', 'dp'), may hold values from -0.109375 to 0.109375
- first_attend: float32 [768, 2304], P('dp', 'mp'), may hold values from -24 to 24
- first_merge: float32 [768, 768], P('dp', 'mp'), may hold values from -14 to 14
- first_norms: float32 [4, 768], P('mp', 'dp'), may hold values from -32 to 32
- first_gate: float32 [768, 3072], P('dp', 'mp'), may hold values from -20 to 20
- first_value: float32 [768, 3072], P('dp', 'mp'), may hold values from -14 to 14
- first_down: float32 [3072, 768], P('mp', 'dp'), may hold values from -28 to 28
- second_attend: float32 [768, 2304], P('dp', 'mp'), may hold values from 1.032192 to 8.84736
- second_merge: float32 [768, 768], P('dp', 'mp'), may hold values from 0.262144 to 2.21184
- second_norms: float32 [4, 768], P('mp', 'dp'), may hold values from 1.572864 to 13.43488
- second_gate: float32 [768, 3072], P('dp', 'mp'), may hold values from 0.606208 to 5.24288
- second_value: float32 [768, 3072], P('dp', 'mp'), may hold values from 0.278528 to 2.359296
- second_down: float32 [3072, 768], P('mp', 'dp'), may hold values from 1.097728 to 9.50272
Outputs:
- layer_output: bfloat16 [16384, 768], P(('dp', 'mp'))
- input_gradient: float32 [16384, 768], P(('dp', 'mp'))
- gradient_attend: float32 [768, 2304], P('dp', 'mp')
- gradient_merge: float32 [768, 768], P('dp', 'mp')
- gradient_norms: float32 [4, 768], P('mp', 'dp')
- gradient_gate: float32 [768, 3072], P('dp', 'mp')
- gradient_value: float32 [768, 3072], P('dp', 'mp')
- gradient_down: float32 [3072, 768], P('mp', 'dp')
- moment_attend: float32 [768, 2304], P('dp', 'mp')
- moment_merge: float32 [768, 768], P('dp', 'mp')
- moment_norms: float32 [4, 768], P('mp', 'dp')
- moment_gate: float32 [768, 3072], P('dp', 'mp')
- moment_value: float32 [768, 3072], P('dp', 'mp')
- moment_down: float32 [3072, 768], P('mp', 'dp')
- squares_attend: float32 [768, 2304], P('dp', 'mp')
- squares_merge: float32 [768, 768], P('dp', 'mp')
- squares_norms: float32 [4, 768], P('mp', 'dp')
- squares_gate: float32 [768, 3072], P('dp', 'mp')
- squares_value: float32 [768, 3072], P('dp', 'mp')
- squares_down: float32 [3072, 768], P('mp', 'dp')
- updated_attend: float32 [768, 2304], P('dp', 'mp')
- updated_merge: float32 [768, 768], P('dp', 'mp')
- updated_norms: float32 [4, 768], P('mp', 'dp')
- updated_gate: float32 [768, 3072], P('dp', 'mp')
- updated_value: float32 [768, 3072], P('dp', 'mp')
- updated_down: float32 [3072, 768], P('mp', 'dp')
Inputs may be any that keep to these rules, and one draw needn't show every extreme that they name: `masked_positions`: each row holds 32 different positions. Slots masked_counts[n] and later of sequence n are not live and are ignored, together with their replace_rows and masked_cotangent entries. Some sequence has exactly 32 live slots and some exactly the least value.
All inputs are finite; a program needn't handle non-finite values.
Results may differ from a plain program's by a relative error of at most 0.013.
The roundings to bfloat16 on the way count: a program that leaves them out, or rounds other values in their place, can miss the bound.
Values may be sent and summed in bfloat16 or wider, within the bound.
No kernel may reach another device: no remote copies, remote signals or barrier semaphores. Data moves between devices by JAX's collectives and lax.ppermute only.
A program may use at most 192 MiB of HBM per device.

v0:
```python
from functools import partial

import jax
import jax.numpy as jnp
from jax import lax
from jax.experimental import pallas as pl
from jax.experimental.pallas import tpu as pltpu
from jax.sharding import PartitionSpec as P

HEADS = 12
HEAD_DIM = 64


beta_one = 0.9
beta_two = 0.999
peak_rate = 1.0
warm_steps = 4.0
total_steps = 100.0
decay_rate = 0.01
adam_eps = 1e-08
norm_eps = 1e-05


def layer_norm(row_data, gain_row, shift_row):
    centered = row_data - jnp.mean(row_data, axis=-1, keepdims=True)
    spread = jnp.mean(centered * centered, axis=-1, keepdims=True)
    return centered * lax.rsqrt(spread + norm_eps) * gain_row + shift_row


def alibi_table(head_count, seq_len):
    slopes = jnp.exp2(-8.0 * jnp.arange(1, head_count + 1, dtype=jnp.float32) / head_count)
    places = jnp.arange(seq_len, dtype=jnp.float32)
    return slopes[:, None, None] * jnp.abs(places[:, None] - places[None, :])


def dot_nn(left_op, right_op):
    return lax.dot_general(
        left_op, right_op, (((1,), (0,)), ((), ())), preferred_element_type=jnp.float32
    )


def dot_nt(left_op, right_op):
    return lax.dot_general(
        left_op, right_op, (((1,), (1,)), ((), ())), preferred_element_type=jnp.float32
    )


def dot_tn(left_op, right_op):
    return lax.dot_general(
        left_op, right_op, (((0,), (0,)), ((), ())), preferred_element_type=jnp.float32
    )


def flip(block, axis, bits):
    size = lax.axis_size(axis)
    return lax.ppermute(block, axis, [(i, i ^ bits) for i in range(size)])


def flip_core(block):
    return flip(block, "mp", 1)


def flip_x(block):
    return flip(block, "mp", 2)


def flip_y(block):
    return flip(block, "dp", 1)


def norm_stats(row_data):
    centered = row_data - jnp.mean(row_data, axis=-1, keepdims=True)
    spread = jnp.mean(centered * centered, axis=-1, keepdims=True)
    inverse = lax.rsqrt(spread + norm_eps)
    return centered * inverse, inverse


def z_groups():
    size = lax.axis_size("dp")
    return [list(range(low, size, 2)) for low in range(2)]


def pass_on(*refs):
    pass


def after(block, *others):
    return pl.pallas_call(
        pass_on,
        out_shape=jax.ShapeDtypeStruct(block.shape, block.dtype),
        in_specs=[pl.BlockSpec(memory_space=pl.ANY)] * (1 + len(others)),
        out_specs=pl.BlockSpec(memory_space=pl.ANY),
        input_output_aliases={0: 0},
        cost_estimate=pl.CostEstimate(flops=0, bytes_accessed=0, transcendentals=0),
    )(block, *others)


def is_small():
    return lax.axis_size("dp") == 8


def gather_z(block):
    far = flip(block, "dp", 4)
    return [block, far, flip(block, "dp", 2), flip(far, "dp", 2)]


def piece_rows(features):
    at = jnp.arange(8, dtype=jnp.int32)
    if is_small():
        along_z = ((at & 1) << 1) + ((at >> 1) & 1)
        at = (2 * along_z + (at >> 2)) ^ lax.axis_index("dp")
    return at * (features // 8)


def gather_whole(block):
    whole = lax.all_gather(block, "dp", axis=1, tiled=True)
    lots, features, columns = whole.shape
    whole = whole.reshape(lots, 8, features // 8, columns).transpose(1, 0, 2, 3)
    return [whole], [flip_x(whole)]


def add_low(*parts):
    return sum(part.astype(jnp.float32) for part in parts).astype(jnp.bfloat16)


def sum_dp(whole):
    return lax.psum_scatter(whole.astype(jnp.float32), "dp", scatter_dimension=0, tiled=True)


def from_pieces(*parts):
    whole = jnp.concatenate(parts, axis=0)
    return sum_dp(whole.reshape(-1, whole.shape[-1]))


MIB = 1024 * 1024
ANYWHERE = pl.BlockSpec(memory_space=pl.ANY)
IN_VMEM = pl.BlockSpec(memory_space=pltpu.VMEM)
IN_SMEM = pl.BlockSpec(memory_space=pltpu.SMEM)


def kernel_call(body, outs, specs, scratch, limit):
    return pl.pallas_call(
        body,
        out_shape=outs,
        in_specs=specs,
        out_specs=[IN_VMEM] * len(outs),
        scratch_shapes=scratch,
        compiler_params=pltpu.CompilerParams(vmem_limit_bytes=limit * MIB),
        cost_estimate=pl.CostEstimate(flops=0, bytes_accessed=0, transcendentals=0),
    )


def like(shape, dtype):
    return jax.ShapeDtypeStruct(shape, dtype)


def with_lot(groups, lot):
    return [(group, (i, lot)) for group in groups for i in range(group.shape[0])]


def load_pieces(pieces, rows, total, sems):
    copies = []
    count = total.shape[0] // 8
    for k, (group, at) in enumerate(pieces):
        to = total.at[pl.ds(pl.multiple_of(rows[k], 32), count), :]
        copies.append(pltpu.make_async_copy(group.at[(*at, pl.ds(0, count))], to, sems.at[k]))
        copies[-1].start()
    return copies


EXTRA = 16


def load_extras(groups, spots, total, sems):
    copies = []
    for group in groups:
        for i in range(group.shape[0]):
            k = len(copies)
            source = group.at[i, 0, pl.ds(group.shape[2] - EXTRA, EXTRA), :]
            copies.append(pltpu.make_async_copy(source, total.at[spots[k]], sems.at[k]))
            copies[-1].start()
    return copies


def split_low(block):
    parts = []
    for _ in range(3):
        part = lax.reduce_precision(block, 8, 7)
        parts.append(jnp.pad(part.astype(jnp.bfloat16), ((0, EXTRA - 1), (0, 128 - block.shape[1]))))
        block = block - part
    return jnp.pad(jnp.concatenate(parts, axis=1), ((0, 0), (0, 384)))


def wait_all(copies):
    for copy in copies:
        copy.wait()


def gelu_parts(gated):
    below = 0.5 + 0.5 * lax.erf(gated * 0.7071067811865476)
    return gated * below, below


def lower_lanes(shape):
    return lax.broadcasted_iota(jnp.int32, shape, 1) < 64


def unpack_columns_of(blocks, attend, merge):
    for block, (column, merge_column) in enumerate(((0, 0), (640, 256), (1152, 384), (1792, 640))):
        attend[:, column : column + 512] = blocks[block, :, :512]
        merge[:, merge_column : merge_column + 128] = blocks[block, :, 512:640]
    for pair, (column, merge_column) in enumerate(((512, 128), (1664, 512))):
        even = blocks[2 * pair, :, 640:].astype(jnp.float32)
        odd = blocks[2 * pair + 1, :, 640:].astype(jnp.float32)
        lower = lower_lanes(even.shape)
        attend[:, column : column + 128] = jnp.where(lower, even, odd).astype(jnp.bfloat16)
        mixed_up = pltpu.roll(jnp.where(lower, odd, even), 64, 1)
        merge[:, merge_column : merge_column + 128] = mixed_up.astype(jnp.bfloat16)


def first_kernel(counts, extra, places, rows, spots, start, norms_given, positions, *refs):
    low = jnp.bfloat16
    groups = []
    for count in counts:
        groups.append(refs[:count])
        refs = refs[count:]
    attend, merge, mixed, normed, *narrow, slot_sum, slot_attended, slot_narrow, norms = refs[:10]
    blocks, attended, scores, extras, sems = refs[10:]
    copies = []
    for at, group in enumerate(groups):
        copies += load_pieces(with_lot(group, 0), rows, blocks.at[places[at]], sems.at[0, at])
        if extra:
            copies += load_extras(group, spots, extras.at[places[at]], sems.at[1, at])
    wait_all(copies)
    if extra:
        for block in range(4):
            whole = jnp.zeros((8, norms.shape[1]), jnp.float32)
            for spot in range(8):
                parts = extras[block, spot].astype(jnp.float32)[:8, :]
                value = parts[:, :128] + parts[:, 128:256] + parts[:, 256:384]
                value = jnp.concatenate([value, jnp.zeros((8, norms.shape[1] - 128), jnp.float32)], axis=1)
                whole = whole + (pltpu.roll(value, spot * (norms.shape[1] // 8), 1) if spot else value)
            norms[block : block + 1, :] = whole[:1, :]
    else:
        norms[...] = norms_given[...]
    unpack_columns_of(blocks, attend, merge)
    width = merge.shape[0]
    length = 128
    slots = 32
    scale = HEAD_DIM ** (-0.5)
    for column in range(0, 3 * width, 256):
        cut = slice(column, column + 256)
        mixed[:, cut] = dot_nn(start[...], attend[:, cut]).astype(low)
    shape = (length, length)
    apart = jnp.abs(
        lax.broadcasted_iota(jnp.int32, shape, 0) - lax.broadcasted_iota(jnp.int32, shape, 1)
    ).astype(jnp.float32)
    lower = lower_lanes(shape)

    def step(target, first, seq, carry):
        at = pl.ds(pl.multiple_of(seq * length, length), length)
        to = pl.ds(pl.multiple_of(seq * slots, slots), slots)
        for pair in range(HEADS // 2):
            column = 2 * HEAD_DIM * pair
            queries = mixed[at, column : column + 128]
            keys = mixed[at, width + column : width + column + 128]
            zero = jnp.zeros_like(queries)
            for half in range(2):
                own = jnp.where(lower, queries, zero) if half == 0 else jnp.where(lower, zero, queries)
                head = 2 * pair + half
                scores[head] = dot_nt(own, keys) * scale - apart * slopes_of(head)
        raised = scores[...]
        raised = jnp.exp(raised - jnp.max(raised, axis=-1, keepdims=True))
        scores[...] = raised / jnp.sum(raised, axis=-1, keepdims=True)
        for pair in range(HEADS // 2):
            column = 2 * HEAD_DIM * pair
            values = mixed[at, 2 * width + column : 2 * width + column + 128]
            heads = [dot_nn(scores[2 * pair + half].astype(low), values) for half in range(2)]
            attended[at, column : column + 128] = jnp.where(lower, heads[0], heads[1]).astype(low)
        total = start[at, :].astype(jnp.float32) + dot_nn(attended[at, :], merge[...])
        xhat, _ = norm_stats(total)
        rows = xhat * norms[0:1, :] + norms[1:2, :]
        normed[at, :] = rows
        target[pl.ds(pl.multiple_of((seq - first) * length, length), length), :] = rows.astype(low)
        selector = one_hot(positions[to, :], length)
        slot_sum[to, :] = select_exact(selector, total)
        slot_attended[to, :] = dot_nn(selector, attended[at, :]).astype(low)
        slot_narrow[to, :] = dot_nn(selector, rows.astype(low)).astype(low)
        return carry

    seqs = start.shape[0] // length // 2
    lax.fori_loop(0, seqs, partial(step, narrow[0], 0), 0, unroll=True)
    lax.fori_loop(seqs, 2 * seqs, partial(step, narrow[1], seqs), 0, unroll=True)


def first_part(extra, places, rows, spots, start, norms, positions, groups):
    count, width = start.shape
    slot_rows = positions.shape[0]
    low = jnp.bfloat16
    return kernel_call(
        partial(first_kernel, [len(group) for group in groups], extra),
        [
            like((width, 3 * width), low),
            like((width, width), low),
            like((count, 3 * width), low),
            like((count, width), jnp.float32),
            like((count // 2, width), low),
            like((count // 2, width), low),
            like((slot_rows, width), jnp.float32),
            like((slot_rows, width), low),
            like((slot_rows, width), low),
            like((4, width), jnp.float32),
        ],
        [IN_SMEM] * 3 + [IN_VMEM] * 3 + [ANYWHERE] * sum(map(len, groups)),
        [
            pltpu.VMEM((4, width, width), low),
            pltpu.VMEM((count, width), low),
            pltpu.VMEM((HEADS, 128, 128), jnp.float32),
            pltpu.VMEM((4, 8, EXTRA, width), low),
            pltpu.SemaphoreType.DMA((2, 4, 8)),
        ], 30)(places, rows, spots, start, norms, positions, *sum(groups, []))


def pack_columns(attend, merge, core_at):
    even = jnp.concatenate(
        [attend[:, :512], merge[:, :128], attend[:, 512:], merge[:, 128:]], axis=1
    )
    odd = jnp.concatenate([attend[:, 64:], merge[:, 64:], merge[:, :64], attend[:, :64]], axis=1)
    return jnp.where(core_at == 0, even, odd)


def unpack_columns(packed, core_at):
    even = jnp.concatenate([packed[:, :512], packed[:, 640:704]], axis=1)
    odd = jnp.concatenate([packed[:, 704:], packed[:, :512]], axis=1)
    even_merge = jnp.concatenate([packed[:, 512:640], packed[:, 704:]], axis=1)
    odd_merge = jnp.concatenate([packed[:, 640:704], packed[:, 512:640]], axis=1)
    return jnp.where(core_at == 0, even, odd), jnp.where(core_at == 0, even_merge, odd_merge)


def front_kernel(count, rows, *refs):
    sources, refs = refs[:4], refs[4:]
    near, far = refs[: count[0]], refs[count[0] : count[0] + count[1]]
    hidden, gates, values, sems = refs[-4:]
    copies = []
    for k, groups in enumerate((near, far)):
        copies.append(
            load_pieces(with_lot(groups, 0), rows, gates.at[k], sems.at[k, 0])
            + load_pieces(with_lot(groups, 1), rows, values.at[k], sems.at[k, 1])
        )
    quarter = sources[0].shape[0]
    for k in range(2):
        wait_all(copies[k])
        for part, source in enumerate(sources):
            start = part * quarter

            def step(tile, carry, k=k, start=start, source=source):
                block = source[pl.ds(pl.multiple_of(tile * 256, 256), 256), :]
                to = pl.ds(pl.multiple_of(start + tile * 256, 256), 256)
                for column in range(0, gates.shape[2], 256):
                    cut = slice(column, column + 256)
                    gated = dot_nn(block, gates[k, :, cut])
                    valued = dot_nn(block, values[k, :, cut])
                    hidden[k, to, cut] = (gelu_parts(gated)[0] * valued).astype(jnp.bfloat16)
                return carry

            lax.fori_loop(0, source.shape[0] // 256, step, 0)


def ffn_front(rows, sources, near, far, *earlier):
    quarter, width = sources[0].shape
    return kernel_call(
        partial(front_kernel, (len(near), len(far))),
        [like((2, 4 * quarter, width), jnp.bfloat16)],
        [IN_SMEM] + [IN_VMEM] * 4 + [ANYWHERE] * (len(near) + len(far) + len(earlier)),
        [
            pltpu.VMEM((2, width, width), jnp.bfloat16),
            pltpu.VMEM((2, width, width), jnp.bfloat16),
            pltpu.SemaphoreType.DMA((2, 2, 8)),
        ], 18)(rows, *sources, *near, *far, *earlier)[0]


def down_kernel(lots, rows, hidden, *refs):
    split, end = len(lots[0]), len(lots[0]) + len(lots[1])
    mine, other, downs, sems = refs[end + 1 :]
    copies = load_pieces(zip(refs[:split], lots[0]), rows, downs.at[0], sems.at[0])
    copies += load_pieces(zip(refs[split:end], lots[1]), rows, downs.at[1], sems.at[1])
    wait_all(copies)
    half = mine.shape[0]
    for part, target in ((1, other), (0, mine)):

        def step(tile, carry, part=part, target=target):
            at = pl.ds(pl.multiple_of(part * half + tile * 256, 256), 256)
            to = pl.ds(pl.multiple_of(tile * 256, 256), 256)
            target[to, :] = dot_nt(hidden[0, at, :], downs[0]) + dot_nt(hidden[1, at, :], downs[1])
            return carry

        lax.fori_loop(0, half // 256, step, 0)


def ffn_down(rows, hidden, near, far, earlier):
    both, width = hidden.shape[1:]
    return kernel_call(
        partial(down_kernel, [[lot for _, lot in group] for group in (near, far)]),
        [like((both // 2, width), jnp.float32)] * 2,
        [IN_SMEM, IN_VMEM] + [ANYWHERE] * (len(near) + len(far) + 1),
        [pltpu.VMEM((2, width, width), jnp.bfloat16), pltpu.SemaphoreType.DMA((2, 8))], 16)(rows, hidden, *[group for group, _ in near + far], earlier)


def select_exact(selector, block):
    first = block.astype(jnp.bfloat16)
    rest = block - first.astype(jnp.float32)
    second = rest.astype(jnp.bfloat16)
    third = (rest - second.astype(jnp.float32)).astype(jnp.bfloat16)
    return dot_nn(selector, first) + dot_nn(selector, second) + dot_nn(selector, third)


def norm_back(xhat, inverse, gain_row, incoming):
    scaled = incoming * gain_row
    inner = jnp.mean(scaled * xhat, axis=-1, keepdims=True)
    back = inverse * (scaled - jnp.mean(scaled, axis=-1, keepdims=True) - xhat * inner)
    gain_back = jnp.sum(incoming * xhat, axis=0, keepdims=True)
    return back, gain_back, jnp.sum(incoming, axis=0, keepdims=True)


def one_hot(positions, length):
    shape = (positions.shape[0], length)
    return (positions == lax.broadcasted_iota(jnp.int32, shape, 1)).astype(jnp.bfloat16)


def second_kernel(
    normed, part, got, norms, positions, live, cotangent, output, pulled, back, norm_grads
):
    slots = cotangent.shape[1]
    length = normed.shape[0] // cotangent.shape[0]
    norm_grads[...] = jnp.zeros_like(norm_grads)

    def step(seq, carry):
        at = pl.ds(pl.multiple_of(seq * length, length), length)
        to = pl.ds(pl.multiple_of(seq * slots, slots), slots)
        total = normed[at, :] + part[at, :] + got[at, :]
        xhat, _ = norm_stats(total)
        output[at, :] = (xhat * norms[2:3, :] + norms[3:4, :]).astype(jnp.bfloat16)
        selector = one_hot(positions[to, :], length)
        xhat, inverse = norm_stats(select_exact(selector, total))
        incoming = jnp.where(live[to, :] > 0, cotangent[seq].astype(jnp.float32), 0.0)
        slot_back, gain_back, shift_back = norm_back(xhat, inverse, norms[2:3, :], incoming)
        back[to, :] = slot_back
        pulled[to, :] = slot_back.astype(jnp.bfloat16)
        norm_grads[0:1, :] += gain_back
        norm_grads[1:2, :] += shift_back
        return carry

    lax.fori_loop(0, cotangent.shape[0], step, 0, unroll=True)


def second_norm(normed, part, got, norms, positions, live, cotangent):
    count, width = normed.shape
    slot_rows = positions.shape[0]
    return kernel_call(
        second_kernel,
        [
            like((count, width), jnp.bfloat16),
            like((slot_rows, width), jnp.bfloat16),
            like((slot_rows, width), jnp.float32),
            like((2, width), jnp.float32),
        ],
        [IN_VMEM] * 7,
        [], 14)(normed, part, got, norms, positions, live, cotangent)


def back_kernel(count, lots, rows, *refs):
    pulls, narrows = refs[0:4], refs[4:8]
    wide, deep = refs[8 : 8 + count[0]], refs[8 + count[0] : 8 + count[0] + count[1]]
    keep, send, pull_rows, work_rows, gate_back, value_back, hidden = refs[
        8 + count[0] + count[1] : -4
    ]
    gates, values, downs, sems = refs[-4:]
    copies = load_pieces(with_lot(wide, 0), rows, gates, sems.at[0])
    copies += load_pieces(with_lot(wide, 1), rows, values, sems.at[1])
    copies += load_pieces(zip(deep, lots), rows, downs, sems.at[2])
    size = pulls[0].shape[0]
    for k in range(4):
        pull_rows[k * size : (k + 1) * size, :] = pulls[k][...]
        work_rows[k * size : (k + 1) * size, :] = narrows[k][...]
    wait_all(copies)
    for column in range(0, gates.shape[1], 256):
        cut = slice(column, column + 256)
        gated = dot_nn(work_rows[...], gates[:, cut])
        valued = dot_nn(work_rows[...], values[:, cut])
        hidden_back = dot_nn(pull_rows[...], downs[:, cut])
        gelu, below = gelu_parts(gated)
        slope = below + gated * (0.3989422804014327 * jnp.exp(-0.5 * gated * gated))
        hidden[:, cut] = (gelu * valued).astype(jnp.bfloat16)
        gate_back[:, cut] = (hidden_back * valued * slope).astype(jnp.bfloat16)
        value_back[:, cut] = (hidden_back * gelu).astype(jnp.bfloat16)
    for column in range(0, gates.shape[0], 256):
        cut = slice(column, column + 256)
        total = dot_nt(gate_back[...], gates[cut, :]) + dot_nt(value_back[...], values[cut, :])
        for k, target in enumerate((keep, keep, send, send)):
            target[k % 2, :, cut] = total[k * size : (k + 1) * size]


def ffn_back(rows, pulls, narrows, wide, deep):
    size, width = pulls[0].shape
    low = jnp.bfloat16
    return kernel_call(
        partial(back_kernel, (len(wide), len(deep)), [lot for _, lot in deep]),
        [like((2, size, width), jnp.float32)] * 2 + [like((4 * size, width), low)] * 5,
        [IN_SMEM] + [IN_VMEM] * 8 + [ANYWHERE] * (len(wide) + len(deep)),
        [pltpu.VMEM((width, width), low)] * 3 + [pltpu.SemaphoreType.DMA((3, 8))], 22)(rows, *pulls, *narrows, *wide, *[group for group, _ in deep])


def store_pieces(total, rows, mine, other):
    count = total.shape[0] // 8
    for k in range(8):
        at = pl.ds(pl.multiple_of(rows[k], 32), count)
        to = mine if k < 4 else other
        to[k % 4, :count, :] = total[at, :]


def grads_kernel(lots, rows, *refs):
    factors, refs = refs[: 2 * lots], refs[-3 - lots :]
    mine, other, total, turned = refs[0], refs[1], refs[2], refs[3:]
    for lot in range(lots):
        turned[lot][...] = factors[2 * lot][...].T
    for lot in range(lots):
        for column in range(0, total.shape[1], 256):
            cut = slice(column, column + 256)
            product = dot_nn(turned[lot][...], factors[2 * lot + 1][:, cut])
            total[:, cut] = product.astype(jnp.bfloat16)
        store_pieces(total, rows, mine.at[:, lot], other.at[:, lot])


def ffn_grads(rows, factors, *earlier):
    size, width = factors[0].shape
    lots = len(factors) // 2
    low = jnp.bfloat16
    return kernel_call(
        partial(grads_kernel, lots),
        [like((4, lots, width // 8, width), low)] * 2,
        [IN_SMEM] + [IN_VMEM] * len(factors) + [ANYWHERE] * len(earlier),
        [pltpu.VMEM((width, width), low)] + [pltpu.VMEM((width, size), low)] * lots, 16)(rows, *factors, *earlier)


def split_kernel(from_y, from_x, *refs):
    first, second, sems = refs[-3:]
    half = first.shape[0]
    copies = [
        pltpu.make_async_copy(from_y.at[pl.ds(0, half)], first, sems.at[0]),
        pltpu.make_async_copy(from_x.at[pl.ds(half, half)], second, sems.at[1]),
    ]
    for copy in copies:
        copy.start()
    wait_all(copies)


def split_halves(from_y, from_x, *earlier):
    half = like((from_y.shape[0] // 2,) + from_y.shape[1:], from_y.dtype)
    return kernel_call(
        split_kernel,
        [half, half],
        [ANYWHERE] * (2 + len(earlier)),
        [pltpu.SemaphoreType.DMA((2,))], 6)(from_y, from_x, *earlier)


def cast_kernel(first, second, _, both):
    both[0] = first[...].astype(jnp.bfloat16)
    both[1] = second[...].astype(jnp.bfloat16)


def cast_wide(first, second, earlier):
    return kernel_call(
        cast_kernel,
        [like((2,) + first.shape, jnp.bfloat16)],
        [IN_VMEM] * 2 + [ANYWHERE],
        [], 4)(first, second, earlier)[0]


def wide_sum(*blocks):
    return sum(block.astype(jnp.float32) for block in blocks)


def total_of(*blocks):
    return wide_sum(*blocks)


def corner_kernel(near, got, *refs):
    first, second = refs[-2:]
    for k in range(4):
        target = first if k < 2 else second
        target[k % 2] = wide_sum(near[k], got[k]).astype(jnp.bfloat16)


def corner_sum(near, got, *earlier):
    half = like((2,) + near.shape[1:], near.dtype)
    return kernel_call(
        corner_kernel, [half, half], [IN_VMEM] * 2 + [ANYWHERE] * len(earlier), [], 6)(near, got, *earlier)


def sides_kernel(near_y, got_y, near_x, got_x, corner_x, corner_y, _, to_x, to_y):
    for k in range(4):
        corner = [corner_x[k]] if k < 2 else []
        to_y[k] = wide_sum(near_y[k], got_y[k], *corner).astype(jnp.bfloat16)
        corner = [corner_y[k - 2]] if k >= 2 else []
        to_x[k] = wide_sum(near_x[k], got_x[k], *corner).astype(jnp.bfloat16)


def sides_sum(near, got, corner_x, corner_y, earlier):
    side = like(near[1].shape, near[1].dtype)
    return kernel_call(sides_kernel, [side, side], [IN_VMEM] * 6 + [ANYWHERE], [], 10)(
        near[1], got[1], near[2], got[2], corner_x, corner_y, earlier
    )


def chip_kernel(near, got, got_x, got_y, _, mine, far, side, last):
    for k, target in enumerate((mine, far, side, last)):
        total = wide_sum(near[k], got[k], got_x[k], got_y[k])
        target[...] = total.astype(target.dtype)


def chip_sum(near, got, got_x, got_y, earlier):
    piece = near.shape[1:]
    mine, far, side, last = kernel_call(
        chip_kernel,
        [like(piece, jnp.float32)] + [like(piece, near.dtype)] * 3,
        [IN_VMEM] * 4 + [ANYWHERE],
        [], 8)(near, got, got_x, got_y, earlier)
    return mine, side, far, last


def halves_kernel(mine, got, *refs):
    keep, send = refs[-2:]
    half = keep.shape[0]
    for k in range(half):
        keep[k] = wide_sum(mine[k], got[k]).astype(keep.dtype)
        send[k] = wide_sum(mine[half + k], got[half + k]).astype(send.dtype)


def halves_sum(mine, got, *earlier):
    half = like((mine.shape[0] // 2,) + mine.shape[1:], mine.dtype)
    return kernel_call(
        halves_kernel, [half, half], [IN_VMEM] * 2 + [ANYWHERE] * len(earlier), [], 8)(mine, got, *earlier)


def row_gradient_kernel(placed, mixed_back, attend, _, output):
    for column in range(0, placed.shape[1], 256):
        cut = slice(column, column + 256)
        output[:, cut] = placed[:, cut] + dot_nt(mixed_back[...], attend[cut, :])


def row_gradient(placed, mixed_back, attend, earlier):
    count, width = placed.shape
    return kernel_call(
        row_gradient_kernel,
        [like(placed.shape, placed.dtype)],
        [IN_VMEM] * 3 + [ANYWHERE],
        [], 14)(placed, mixed_back, attend, earlier)[0]


def slopes_of(head):
    return 2.0 ** (-8.0 * (head + 1) / HEADS)


def attend_kernel(
    extra,
    rows,
    columns,
    spots,
    second_grads,
    keep,
    got,
    second_back,
    slot_sum,
    norms,
    merge,
    mixed,
    slot_attended,
    start,
    positions,
    _,
    placed,
    mixed_back,
    norm_grads,
    *refs,
):
    near, far = refs[0:4], refs[4:8]
    merge_grad, total, branch, attended_back, first_back, turned, extras = refs[8:]
    width = norms.shape[1]
    slots = 32
    length = 128
    low = jnp.bfloat16
    scale = HEAD_DIM ** (-0.5)
    xhat, inverse = norm_stats(slot_sum[...])
    incoming = keep[...] + got[...].astype(jnp.float32) + second_back[...]
    slot_back, gain_back, shift_back = norm_back(xhat, inverse, norms[0:1, :], incoming)
    norm_grads[0:1, :] = gain_back
    norm_grads[1:2, :] = shift_back
    if extra:
        both = [gain_back, shift_back, second_grads[0:1, :], second_grads[1:2, :]]
        zero_rows = jnp.zeros((EXTRA - 1, width), jnp.float32)
        for block in range(4):
            whole = jnp.concatenate([both[block], zero_rows], axis=0)
            for spot in range(8):
                turn = (8 - spot) % 8 * (width // 8)
                extras[block, spot] = (pltpu.roll(whole, turn, 1) if turn else whole).astype(low)
    first_back[...] = slot_back
    branch[...] = slot_back.astype(low)
    attended_back[...] = dot_nt(branch[...], merge[...]).astype(low)
    merge_grad[...] = dot_tn(slot_attended[...], branch[...])
    lane_head = lax.broadcasted_iota(jnp.int32, (slots, width), 1) // HEAD_DIM

    def apart_heads(block):
        zero = jnp.zeros_like(block)
        return jnp.concatenate(
            [jnp.where(lane_head == head, block, zero) for head in range(HEADS)], axis=0
        )

    def join_heads(block):
        total = jnp.zeros((slots, width), jnp.float32)
        for head in range(HEADS):
            total = jnp.where(lane_head == head, block[head * slots : (head + 1) * slots], total)
        return total

    def step(seq, carry):
        at = pl.ds(pl.multiple_of(seq * length, length), length)
        to = pl.ds(pl.multiple_of(seq * slots, slots), slots)
        spots = positions[to, :]
        selector = one_hot(spots, length)
        apart = jnp.abs(
            spots - lax.broadcasted_iota(jnp.int32, (slots, length), 1)
        ).astype(jnp.float32)
        keys = mixed[at, width : 2 * width]
        values = mixed[at, 2 * width :]
        queries = apart_heads(dot_nn(selector, mixed[at, :width])).astype(low)
        heads_back = apart_heads(attended_back[to, :].astype(jnp.float32)).astype(low)
        bias = jnp.concatenate([apart * slopes_of(head) for head in range(HEADS)], axis=0)
        scores = dot_nt(queries, keys) * scale - bias
        exp_scores = jnp.exp(scores - jnp.max(scores, axis=-1, keepdims=True))
        probs = exp_scores / jnp.sum(exp_scores, axis=-1, keepdims=True)
        probs_back = dot_nt(heads_back, values)
        inner = jnp.sum(probs * probs_back, axis=-1, keepdims=True)
        scores_back = (probs * (probs_back - inner)).astype(low)
        queries_back = (join_heads(dot_nn(scores_back, keys)) * scale).astype(low)
        mixed_back[at, :width] = dot_tn(selector, queries_back).astype(low)
        mixed_back[at, width : 2 * width] = (dot_tn(scores_back, queries) * scale).astype(low)
        mixed_back[at, 2 * width :] = dot_tn(probs.astype(low), heads_back).astype(low)
        spread = (spots == lax.broadcasted_iota(jnp.int32, (slots, length), 1)).astype(jnp.float32)
        placed[at, :] = select_exact(jnp.transpose(spread).astype(low), first_back[to, :])
        return carry

    lax.fori_loop(0, mixed.shape[0] // length, step, 0, unroll=True)
    turned[...] = start[...].T
    for core, target in ((1, far), (0, near)):
        for k in range(2):
            base = 6 * (2 * core + k)
            for part in range(2):
                column = pl.ds(pl.multiple_of(columns[base] + 256 * part, 128), 256)
                product = dot_nn(turned[...], mixed_back[:, column])
                total[:, 256 * part : 256 * part + 256] = product.astype(low)
            column = pl.ds(pl.multiple_of(columns[base + 1], 128), 128)
            total[:, 512:640] = merge_grad[:, column].astype(low)
            column = pl.ds(pl.multiple_of(columns[base + 2], 128), 128)
            single = dot_nn(turned[...], mixed_back[:, column])
            column = pl.ds(pl.multiple_of(columns[base + 3], 128), 128)
            merged = pltpu.roll(merge_grad[:, column], 64, 1)
            attend_lane = lower_lanes(single.shape) == (columns[base + 4] == 0)
            total[:, 640:] = jnp.where(attend_lane, single, merged).astype(low)
            sides = target[2 * k : 2 * k + 2]
            store_pieces(total, rows, *sides)
            if extra:
                for j in range(8):
                    sides[j // 4][j % 4, width // 8 :, :] = extras[columns[base + 5], spots[j]]


def attend_back(extra, rows, columns, spots, second_grads, *blocks):
    start, mixed = blocks[8], blocks[6]
    count, width = start.shape
    slot_rows = blocks[0].shape[0]
    low = jnp.bfloat16
    return kernel_call(
        partial(attend_kernel, extra),
        [
            like((count, width), jnp.float32),
            like(mixed.shape, low),
            like((2, width), jnp.float32),
        ]
        + [like((4, width // 8 + (EXTRA if extra else 0), width), low)] * 8,
        [IN_SMEM] * 3 + [IN_VMEM] * 11 + [ANYWHERE],
        [
            pltpu.VMEM((width, width), jnp.float32),
            pltpu.VMEM((width, width), low),
            pltpu.VMEM((slot_rows, width), low),
            pltpu.VMEM((slot_rows, width), low),
            pltpu.VMEM((slot_rows, width), jnp.float32),
            pltpu.VMEM((width, count), low),
            pltpu.VMEM((4, 8, EXTRA, width), low),
        ], 32)(rows, columns, spots, second_grads, *blocks)


def adamw_step(master, first, second, gradient, step_value, decay):
    step_rate = peak_rate * jnp.minimum(
        step_value / warm_steps, (total_steps - step_value) / (total_steps - warm_steps)
    )
    fix_one = 1.0 - jnp.power(jnp.float32(beta_one), step_value)
    fix_two = 1.0 - jnp.power(jnp.float32(beta_two), step_value)
    moment = beta_one * first + (1.0 - beta_one) * gradient
    squares = beta_two * second + (1.0 - beta_two) * gradient * gradient
    updated = master - step_rate * (
        moment / fix_one / (jnp.sqrt(squares / fix_two) + adam_eps) + decay * master
    )
    return (moment, squares, updated)


def shards(
    hidden_rows,
    token_table,
    masked_positions,
    masked_counts,
    replace_rows,
    masked_cotangent,
    step_number,
    attend_master,
    merge_master,
    norms_master,
    gate_master,
    value_master,
    down_master,
    first_attend,
    first_merge,
    first_norms,
    first_gate,
    first_value,
    first_down,
    second_attend,
    second_merge,
    second_norms,
    second_gate,
    second_value,
    second_down,
):
    local_seqs, slot_count = masked_positions.shape
    local_rows, model_width = hidden_rows.shape
    length = local_rows // local_seqs
    slot_rows = local_seqs * slot_count
    dp_size = lax.axis_size("dp")
    core_at = lax.axis_index("mp") & 1
    x_at = lax.axis_index("mp") >> 1
    low = jnp.bfloat16
    rows = piece_rows(model_width)

    packed = pack_columns(attend_master.astype(low), merge_master.astype(low), core_at)[None]
    small = is_small()
    deep = down_master.astype(low).T[None]

    order = [(core, k) for core in range(2) for k in range(2)]
    places = [2 * (x_at ^ k) + (core_at ^ core) for core, k in order]
    table = jnp.array(
        [
            [0, 0, 512, 128, 0, 0],
            [640, 256, 512, 128, 1, 1],
            [1152, 384, 1664, 512, 0, 2],
            [1792, 640, 1664, 512, 1, 3],
        ],
        jnp.int32,
    )
    columns = jnp.concatenate([table[place] for place in places])
    places = jnp.stack(places).astype(jnp.int32)
    spots = piece_rows(8)
    if small:
        packed = jnp.concatenate([packed, split_low(norms_master)[None]], axis=1)
        packed_z = [packed] + [flip(packed, "dp", 2 * k) for k in (2, 1, 3)]
        wide = cast_wide(gate_master, value_master, packed_z[2])

    live_slots = jnp.arange(slot_count, dtype=jnp.int32)[None, :] < masked_counts[:, None]
    at_slot = masked_positions[:, :, None] == jnp.arange(length, dtype=jnp.int32)[None, None, :]
    place_bool = at_slot & live_slots[:, :, None]
    chosen = jnp.take(token_table, replace_rows.reshape(-1), axis=0).reshape(
        local_seqs, slot_count, model_width
    )
    swapped = jnp.einsum(
        "sjt,sjd->std", place_bool.astype(low), chosen, preferred_element_type=jnp.float32
    ).astype(low)
    replaced = jnp.any(place_bool, axis=1)[:, :, None]
    start_rows = jnp.where(
        replaced, swapped, hidden_rows.reshape(local_seqs, length, model_width)
    ).reshape(local_rows, model_width)
    positions = masked_positions.reshape(slot_rows, 1)
    live = live_slots.astype(jnp.float32).reshape(slot_rows, 1)
    indices = [rows, places, columns, spots, positions, live]
    if small:
        deep = after(deep, start_rows)
        deep_y, deep_x = flip_y(deep), flip_x(deep)
        deep_parts = jnp.concatenate([deep, deep_y, deep_x, flip_x(deep_y)])
        packed_z[0] = after(packed_z[0], wide, deep_parts, *indices)
        wide_z = gather_z(after(wide, packed_z[1], packed_z[3]))
        packed_z = jnp.stack(packed_z)
        packed_y, packed_x = flip_y(packed_z), flip_x(packed_z)
        first_half, second_half = split_halves(packed_y, packed_x, wide_z[1], wide_z[2])
        packed_near = [packed_z, packed_y]
        packed_far = [packed_x, flip_x(first_half), flip_y(second_half)]
        wide_z[0] = after(wide_z[0], *packed_far[1:])
        deep_z = gather_z(after(deep_parts, *wide_z[1:])[None])
        wide_z = jnp.stack(wide_z)
        wide_y, wide_x = flip_y(wide_z), flip_x(wide_z)
        norms = jnp.zeros((4, model_width), jnp.float32)
    else:
        packed_near, packed_far = gather_whole(packed)
        norms = lax.all_gather(norms_master, "dp", axis=1, tiled=True)
        norms = lax.all_gather(norms, "mp", axis=0, tiled=True)

    packed_groups = [packed_near, packed_far]
    packed_groups += [[flip_core(part) for part in group] for group in packed_groups]
    (
        attend_full,
        merge_full,
        mixed,
        normed,
        narrow,
        narrow_end,
        slot_sum,
        slot_attended,
        slot_narrow,
        norms,
    ) = first_part(
        small,
        places,
        rows,
        spots,
        start_rows,
        norms,
        positions,
        packed_groups,
    )
    if small:
        first_half, second_half = split_halves(wide_y, wide_x, narrow, deep_z[2])
        wide_near = [wide_z, wide_y]
        wide_far = [wide_x, flip_x(first_half), flip_y(second_half)]
        deep_near = [(part, (0, side)) for side in (0, 1) for part in deep_z]
        deep_far = [(part, (0, side)) for side in (2, 3) for part in deep_z]
    else:
        wide_near, wide_far = gather_whole(
            jnp.stack([gate_master.astype(low), value_master.astype(low)])
        )
        deep_near, deep_far = (with_lot(group, 0) for group in gather_whole(deep))

    def over_group(block):
        other_x = flip_x(block)
        return [block, other_x, flip_core(block), flip_core(other_x)]


    chip_rows = (narrow, narrow_end, flip_core(narrow), flip_core(narrow_end))
    earlier = [deep_z[1] if small else rows]
    hidden = ffn_front(rows, chip_rows, wide_near, wide_far, *earlier)
    narrows = over_group(after(slot_narrow, hidden))
    ffn_mine, ffn_other = ffn_down(rows, hidden, deep_near, deep_far, rows)
    layer_output, pulled, second_back, second_grads = second_norm(
        normed, ffn_mine, flip_core(ffn_other), norms, positions, live, masked_cotangent
    )

    keep, send, *factors = ffn_back(rows, over_group(pulled), narrows, wide_near, deep_near)
    pull_rows, work_rows, gate_back, value_back, slot_hidden = factors
    chip_back = keep + flip_core(send)
    pair_own, pair_far = ffn_grads(rows, (pull_rows, slot_hidden, work_rows, gate_back))
    value_own, value_far = ffn_grads(rows, (work_rows, value_back), pair_own)
    if small:
        pair_got = flip_y(pair_far)
    placed, mixed_back, first_grads, *parts = attend_back(
        small,
        rows,
        columns,
        spots,
        second_grads,
        chip_back[0],
        flip_x(chip_back[1].astype(low)),
        second_back,
        slot_sum,
        norms,
        merge_full,
        mixed,
        slot_attended,
        start_rows,
        positions,
        value_far,
    )
    near, far = parts[:4], parts[4:]
    got = [flip_core(part) for part in far]
    if small:
        value_got = flip_y(value_far)
        corner_a, corner_b = corner_sum(near[3], got[3], *got[:3])
        corner_x, corner_y = flip_x(corner_a), flip_y(corner_b)
        pair_keep, pair_send = halves_sum(pair_own, pair_got, corner_a)
        pair_back = flip(pair_send, "dp", 2)
        to_x, to_y = sides_sum(near, got, corner_x, corner_y, value_got)
        got_x, got_y = flip_x(to_x), flip_y(to_y)
        value_keep, value_send = halves_sum(value_own, value_got, to_x)
        value_back = flip(value_send, "dp", 2)
        pair_keep, pair_send = halves_sum(pair_keep, pair_back, value_send)
        pair_last = flip(pair_send[0], "dp", 4)
        input_gradient = row_gradient(placed, mixed_back, attend_full, pair_send)
        value_keep, value_send = halves_sum(value_keep, value_back, input_gradient)
        value_last = flip(value_send[0], "dp", 4)
        mine, *sent = chip_sum(near[0], got[0], got_x, got_y, input_gradient)
        pair_grad = total_of(pair_keep[0], after(pair_last, mine))
        gradient_value = total_of(value_keep[0], after(value_last, mine))[0]
        packed_grad = total_of(mine, *[flip(sent[k - 1], "dp", 2 * k) for k in (1, 2, 3)])
        gradient_down, gradient_gate = pair_grad[0].T, pair_grad[1]
    else:
        here, across_y, across_x, corner = (add_low(near[k], got[k]) for k in range(4))
        input_gradient = row_gradient(placed, mixed_back, attend_full, placed)
        gradient_down = from_pieces(pair_own[:, 0], pair_far[:, 0]).T
        gradient_gate = from_pieces(pair_own[:, 1], pair_far[:, 1])
        gradient_value = from_pieces(value_own[:, 0], value_far[:, 0])
        packed_grad = from_pieces(
            add_low(here, flip_x(across_x)), add_low(across_y, flip_x(corner))
        )
    own_rows = attend_master.shape[0]
    gradient_attend, gradient_merge = unpack_columns(packed_grad[:own_rows], core_at)
    if small:
        gradient_norms = packed_grad[own_rows : own_rows + 1, :own_rows]
    else:
        norm_parts = jnp.concatenate([first_grads, second_grads], axis=0)
        gradient_norms = lax.psum_scatter(norm_parts, "mp", scatter_dimension=0, tiled=True)
        gradient_norms = lax.psum_scatter(gradient_norms, "dp", scatter_dimension=1, tiled=True)

    step_value = step_number[0].astype(jnp.float32)
    moment_attend, squares_attend, updated_attend = adamw_step(
        attend_master, first_attend, second_attend, gradient_attend, step_value, decay_rate
    )
    moment_merge, squares_merge, updated_merge = adamw_step(
        merge_master, first_merge, second_merge, gradient_merge, step_value, decay_rate
    )
    moment_norms, squares_norms, updated_norms = adamw_step(
        norms_master, first_norms, second_norms, gradient_norms, step_value, 0.0
    )
    moment_gate, squares_gate, updated_gate = adamw_step(
        gate_master, first_gate, second_gate, gradient_gate, step_value, decay_rate
    )
    moment_value, squares_value, updated_value = adamw_step(
        value_master, first_value, second_value, gradient_value, step_value, decay_rate
    )
    moment_down, squares_down, updated_down = adamw_step(
        down_master, first_down, second_down, gradient_down, step_value, decay_rate
    )
    return (
        layer_output,
        input_gradient,
        gradient_attend,
        gradient_merge,
        gradient_norms,
        gradient_gate,
        gradient_value,
        gradient_down,
        moment_attend,
        moment_merge,
        moment_norms,
        moment_gate,
        moment_value,
        moment_down,
        squares_attend,
        squares_merge,
        squares_norms,
        squares_gate,
        squares_value,
        squares_down,
        updated_attend,
        updated_merge,
        updated_norms,
        updated_gate,
        updated_value,
        updated_down,
    )


def solution(mesh):
    return jax.shard_map(
        shards,
        mesh=mesh,
        in_specs=(
            P(("dp", "mp"), None),
            P(),
            P(("dp", "mp"), None),
            P(("dp", "mp")),
            P(("dp", "mp"), None),
            P(("dp", "mp"), None, None),
            P(),
            P("dp", "mp"),
            P("dp", "mp"),
            P("mp", "dp"),
            P("dp", "mp"),
            P("dp", "mp"),
            P("mp", "dp"),
            P("dp", "mp"),
            P("dp", "mp"),
            P("mp", "dp"),
            P("dp", "mp"),
            P("dp", "mp"),
            P("mp", "dp"),
            P("dp", "mp"),
            P("dp", "mp"),
            P("mp", "dp"),
            P("dp", "mp"),
            P("dp", "mp"),
            P("mp", "dp"),
        ),
        out_specs=(
            P(("dp", "mp"), None),
            P(("dp", "mp"), None),
            P("dp", "mp"),
            P("dp", "mp"),
            P("mp", "dp"),
            P("dp", "mp"),
            P("dp", "mp"),
            P("mp", "dp"),
            P("dp", "mp"),
            P("dp", "mp"),
            P("mp", "dp"),
            P("dp", "mp"),
            P("dp", "mp"),
            P("mp", "dp"),
            P("dp", "mp"),
            P("dp", "mp"),
            P("mp", "dp"),
            P("dp", "mp"),
            P("dp", "mp"),
            P("mp", "dp"),
            P("dp", "mp"),
            P("dp", "mp"),
            P("mp", "dp"),
            P("dp", "mp"),
            P("dp", "mp"),
            P("mp", "dp"),
        ),
        check_vma=False,
    )
```

profile of v0, /device:TPU:0, one launch (start us, length us, event | category | flops | bytes accessed | tf_op | source)
XLA Modules:
  0.0 245.2 jit_solution(18133116001957236130)
XLA Ops:
  3.0 5.1 %collective-permute-start.5 = (bf16[1,112,768]{2,1,0:T(8,128)(2,1)S(1)}, bf16[1,112,768]{2,1,0:T(8,128)(2,1)S(1)}, u32[]{:S(2)}, u32[]{:S(2)}) collective-permute-start(bf16[1,112,768]{2,1,0:T(8,128)(2,1)S(1)} %pad_maximum_fusion.3.refs_0_), channel_id=1, source_target_pairs={{0,24},{4,28},{8,16},{12,20},{16,8},{20,12},{24,0},{28,4},{1,25},{... | collective-permute-start | bytes 516104 | tf_op jit(solution)/shard_map/ppermute | solution.py:56
  9.8 4.6 %gather_fusion = bf16[128,768]{1,0:T(8,128)(2,1)S(1)} fusion(bf16[4096,768]{1,0:T(8,128)(2,1)} %param.27, s32[1024]{0:T(1024)S(1)} %pad_clamp_fusion), kind=kCustom, calls=%fused_computation | custom fusion | bytes 393728 | tf_op jit(solution)/shard_map/jit(_take)/gather | solution.py:877
  14.4 1.4 fusion
  15.9 1.7 collective-permute-start.1
  17.5 1.5 collective-permute-start.2
  20.1 1.2 collective-permute-done.1
  21.2 1.6 collective-permute-start.3
  27.3 1.1 pad_maximum_fusion.1.refs_0_
  28.4 1.7 collective-permute-start.6
  30.2 1.5 collective-permute-start.7
  31.7 2.1 collective-permute-start.8
  33.8 2.0 collective-permute-start.9
  35.8 8.9 %collective-permute-done.8.refs_0_.refs_1_ = bf16[2,96,768]{2,1,0:T(8,128)(2,1)S(1)} collective-permute-done((bf16[2,96,768]{2,1,0:T(8,128)(2,1)}, bf16[2,96,768]{2,1,0:T(8,128)(2,1)S(1)}, u32[]{:S(2)}, u32[]{:S(2)}) %collective-permute-start.8) | collective-permute-done | bytes 294944 | tf_op jit(solution)/shard_map/ppermute | solution.py:56
  45.1 1.1 shard_map.453
  46.2 1.1 collective-permute-start.10
  48.3 1.3 collective-permute-start.19
  50.0 4.9 %collective-permute-done.10.refs_3_.refs_1_ = bf16[2,1,112,768]{3,2,1,0:T(8,128)(2,1)} collective-permute-done((bf16[2,1,112,768]{3,2,1,0:T(8,128)(2,1)S(1)}, bf16[2,1,112,768]{3,2,1,0:T(8,128)(2,1)}, u32[]{:S(2)}, u32[]{:S(2)}) %collective-permute-start.10) | collective-permute-done | bytes 344096 | tf_op jit(solution)/shard_map/ppermute | solution.py:56
  54.9 1.1 collective-permute-done.11.refs_4_.refs_2_
  56.8 2.2 pad_maximum_fusion.refs_4_.refs_8_
  59.4 1.5 collective-permute-start.21
  61.5 3.3 %collective-permute-start.25 = (bf16[1,4,96,768]{3,2,1,0:T(8,128)(2,1)}, bf16[1,4,96,768]{3,2,1,0:T(8,128)(2,1)S(1)}, u32[]{:S(2)}, u32[]{:S(2)}) collective-permute-start(bf16[1,4,96,768]{3,2,1,0:T(8,128)(2,1)} %bitcast.76), channel_id=1, source_target_pairs={{0,16},{4,20},{8,24},{12,28},{16,0},{20,4},{24,8},{28,12},{1,17},{... | collective-permute-start | bytes 1769480 | tf_op jit(solution)/shard_map/ppermute | solution.py:56
  64.8 1.6 collective-permute-done.16.refs_9_
  69.5 11.8 %shard_map.454 = (bf16[768,2304]{1,0:T(8,128)(2,1)S(1)}, bf16[768,768]{1,0:T(8,128)(2,1)S(1)}, bf16[512,2304]{1,0:T(8,128)(2,1)S(1)}, f32[512,768]{1,0:T(8,128)S...) custom-call(s32[4]{0:T(128)S(1)} %copy-done.43, ...), custom_call_target="tpu_custom_call" | custom-call | tf_op jit(solution)/shard_map/pallas_call | solution.py:300
  81.3 1.8 copy-done.8
  83.1 1.4 copy-done.16
  86.8 2.4 collective-permute-done.22.refs_1_.refs_2_.refs_6_.refs_10_.refs_14_.refs_12_.refs_16_
  89.3 1.5 shard_map.457
  91.4 1.7 collective-permute-start.24
  93.6 1.2 collective-permute-done.17.refs_2_
  95.4 10.3 %collective-permute-done.23.refs_7_ = bf16[2,2,96,768]{3,2,1,0:T(8,128)(2,1)S(1)} collective-permute-done((bf16[2,2,96,768]{3,2,1,0:T(8,128)(2,1)S(1)}, bf16[2,2,96,768]{3,2,1,0:T(8,128)(2,1)S(1)}, u32[]{:S(2)}, u32[]{:S(2)}) %collective-permute-start.23) | collective-permute-done | bytes 589856 | tf_op jit(solution)/shard_map/ppermute | solution.py:56
  106.0 1.3 copy-done.7
  107.3 9.3 %shard_map.458.hidden.refs_1_ = bf16[2,1024,768]{2,1,0:T(8,128)(2,1)S(1)} custom-call(s32[8]{0:T(128)S(1)} %copy-done.41, bf16[256,768]{1,0:T(8,128)(2,1)S(1)} %get-tuple-element.86.refs_0_, bf16[256,768]{1,0:T(8,128)(2,1)S(1)} %get-tuple-element.87.refs_1_, bf16[256,768]{1,0:T(8,128)(2,1)S(1)} %collective-permute-done.17.refs_2_, ...), custom_call_target="tpu_custom_call" | custom-call | tf_op jit(solution)/shard_map/pallas_call | solution.py:371
  116.6 7.6 %shard_map.459 = (f32[512,768]{1,0:T(8,128)S(1)}, f32[512,768]{1,0:T(8,128)}) custom-call(s32[8]{0:T(128)S(1)} %copy-done.41, bf16[2,1024,768]{2,1,0:T(8,128)(2,1)S(1)} %shard_map.458.hidden.refs_1_, bf16[1,4,96,768]{3,2,1,0:T(8,128)(2,1)S(1)} %bitcast.77, ...), custom_call_target="tpu_custom_call" | custom-call | tf_op jit(solution)/shard_map/pallas_call | solution.py:402
  124.2 1.1 copy-done.21
  125.4 1.5 collective-permute-start.31
  126.9 2.2 collective-permute-done.27.got
  129.1 1.4 copy-done.20
  130.5 1.4 copy-done.22
  131.9 3.8 %shard_map.460 = (bf16[512,768]{1,0:T(8,128)(2,1)}, bf16[128,768]{1,0:T(8,128)(2,1)S(1)}, f32[128,768]{1,0:T(8,128)S(1)}, f32[2,768]{1,0:T(2,128)S(1)}) custom-call(f32[512,768]{1,0:T(8,128)S(1)} %copy-done.20, f32[512,768]{1,0:T(8,128)S(1)} %copy-done.22, f32[512,768]{1,0:T(8,128)} %collective-permute-done.27.got, f32[4,768]{1,0:T(4,128)S(1)} %copy-done.40, ...), custom_call_target="tpu_custom_call" | custom-call | tf_op jit(solution)/shard_map/pallas_call | solution.py:459
  135.8 1.5 collective-permute-start.28
  137.8 4.9 %collective-permute-done.28.refs_1_ = bf16[128,768]{1,0:T(8,128)(2,1)S(1)} collective-permute-done((bf16[128,768]{1,0:T(8,128)(2,1)S(1)}, bf16[128,768]{1,0:T(8,128)(2,1)S(1)}, u32[]{:S(2)}, u32[]{:S(2)}) %collective-permute-start.28) | collective-permute-done | bytes 196640 | tf_op jit(solution)/shard_map/ppermute | solution.py:56
  142.7 1.4 collective-permute-done.30.refs_3_
  144.1 6.6 %shard_map.462 = (f32[2,128,768]{2,1,0:T(8,128)S(1)}, f32[2,128,768]{2,1,0:T(8,128)S(1)}, bf16[512,768]{1,0:T(8,128)(2,1)S(1)}, bf16[512,768]{1,0:T(8,128)(2,1)S...) custom-call(s32[8]{0:T(128)S(1)} %copy-done.42, ...), custom_call_target="tpu_custom_call" | custom-call | tf_op jit(solution)/shard_map/pallas_call | solution.py:506
  150.9 2.1 shard_map.463
  153.0 1.8 collective-permute-start.36
  154.8 1.4 shard_map.464
  157.1 6.3 %collective-permute-done.35.got = bf16[128,768]{1,0:T(8,128)(2,1)S(1)} collective-permute-done((bf16[128,768]{1,0:T(8,128)(2,1)S(1)}, bf16[128,768]{1,0:T(8,128)(2,1)S(1)}, u32[]{:S(2)}, u32[]{:S(2)}) %collective-permute-start.35) | collective-permute-done | bytes 196640 | tf_op jit(solution)/shard_map/ppermute | solution.py:56
  163.4 11.1 %shard_map.465 = (f32[512,768]{1,0:T(8,128)S(1)}, bf16[512,2304]{1,0:T(8,128)(2,1)S(1)}, f32[2,768]{1,0:T(2,128)}, bf16[4,112,768]{2,1,0:T(8,128)(2,1)S(1)}, bf1...) custom-call(s32[8]{0:T(128)S(1)} %copy-done.42, ...), custom_call_target="tpu_custom_call" | custom-call | tf_op jit(solution)/shard_map/pallas_call | solution.py:780
  175.5 1.1 collective-permute-done.37.got
  180.4 1.2 collective-permute-start.44
  182.3 12.3 %collective-permute-done.42._.got = bf16[4,1,96,768]{3,2,1,0:T(8,128)(2,1)S(1)} collective-permute-done((bf16[4,1,96,768]{3,2,1,0:T(8,128)(2,1)S(1)}, bf16[4,1,96,768]{3,2,1,0:T(8,128)(2,1)S(1)}, u32[]{:S(2)}, u32[]{:S(2)}) %collective-permute-start.42) | collective-permute-done | bytes 589856 | tf_op jit(solution)/shard_map/ppermute | solution.py:56
  194.6 6.8 %collective-permute-done.44.corner_y = bf16[2,112,768]{2,1,0:T(8,128)(2,1)S(1)} collective-permute-done((bf16[2,112,768]{2,1,0:T(8,128)(2,1)S(1)}, bf16[2,112,768]{2,1,0:T(8,128)(2,1)S(1)}, u32[]{:S(2)}, u32[]{:S(2)}) %collective-permute-start.44) | collective-permute-done | bytes 344096 | tf_op jit(solution)/shard_map/ppermute | solution.py:56
  201.8 1.5 collective-permute-start.45
  204.5 2.2 collective-permute-start.50
  207.4 3.2 %shard_map.471._.refs_0_ = f32[512,768]{1,0:T(8,128)} custom-call(f32[512,768]{1,0:T(8,128)S(1)} %get-tuple-element.111.placed, bf16[512,2304]{1,0:T(8,128)(2,1)S(1)} %get-tuple-element.112.mixed_back, bf16[768,2304]{1,0:T(8,128)(2,1)S(1)} %copy-done.9, bf16[1,2,96,768]{3,2,1,0:T(8,128)(2,1)S(1)} %get-tuple-element.129._), custom_call_target="tpu_custom_call" | custom-call | tf_op jit(solution)/shard_map/pallas_call | solution.py:653
  210.6 6.7 %collective-permute-done.51.got = bf16[2,1,96,768]{3,2,1,0:T(8,128)(2,1)S(1)} collective-permute-done((bf16[2,1,96,768]{3,2,1,0:T(8,128)(2,1)S(1)}, bf16[2,1,96,768]{3,2,1,0:T(8,128)(2,1)S(1)}, u32[]{:S(2)}, u32[]{:S(2)}) %collective-permute-start.51) | collective-permute-done | bytes 294944 | tf_op jit(solution)/shard_map/ppermute | solution.py:56
  217.3 1.4 copy-done.2
  221.2 2.2 collective-permute-start.49
  224.2 1.4 collective-permute-start.47
  227.4 1.1 multiply_subtract_fusion.2
  229.9 4.9 %collective-permute-done.52.refs_0_ = bf16[1,96,768]{2,1,0:T(8,128)(2,1)S(1)} collective-permute-done((bf16[1,96,768]{2,1,0:T(8,128)(2,1)S(1)}, bf16[1,96,768]{2,1,0:T(8,128)(2,1)S(1)}, u32[]{:S(2)}, u32[]{:S(2)}) %collective-permute-start.52) | collective-permute-done | bytes 147488 | tf_op jit(solution)/shard_map/ppermute | solution.py:56
  235.4 2.0 multiply_subtract_fusion.1
  237.5 4.3 %collective-permute-done.48 = bf16[112,768]{1,0:T(8,128)(2,1)S(1)} collective-permute-done((bf16[112,768]{1,0:T(8,128)(2,1)S(1)}, bf16[112,768]{1,0:T(8,128)(2,1)S(1)}, u32[]{:S(2)}, u32[]{:S(2)}) %collective-permute-start.48) | collective-permute-done | bytes 172064 | tf_op jit(solution)/shard_map/ppermute | solution.py:56
  242.6 1.2 multiply_subtract_fusion.3
  (266 shorter events, 37.5 us)
Async XLA Ops:
  3.0 12.8 %copy-start.47 = (bf16[1,112,768]{2,1,0:T(8,128)(2,1)}, bf16[1,112,768]{2,1,0:T(8,128)(2,1)S(1)}, u32[]{:S(2)}) copy-start(bf16[1,112,768]{2,1,0:T(8,128)(2,1)S(1)} %pad_maximum_fusion.3.refs_0_) | copy-start | bytes 516100
  3.0 11.3 %copy-start.54 = (bf16[512,768]{1,0:T(8,128)(2,1)S(1)}, bf16[512,768]{1,0:T(8,128)(2,1)}, u32[]{:S(2)}) copy-start(bf16[512,768]{1,0:T(8,128)(2,1)} %param.26) | copy-start | bytes 2359300
  3.0 24.2 %collective-permute-start.5 = (bf16[1,112,768]{2,1,0:T(8,128)(2,1)S(1)}, bf16[1,112,768]{2,1,0:T(8,128)(2,1)S(1)}, u32[]{:S(2)}, u32[]{:S(2)}) collective-permute-start(bf16[1,112,768]{2,1,0:T(8,128)(2,1)S(1)} %pad_maximum_fusion.3.refs_0_), channel_id=1, source_target_pairs={{0,24},{4,28},{8,16},{12,20},{16,8},{20,12},{24,0},{28,4},{1,25},{... | collective-permute-start | bytes 516104 | tf_op jit(solution)/shard_map/ppermute | solution.py:56
  8.2 17.3 %collective-permute-start = (bf16[1,112,768]{2,1,0:T(8,128)(2,1)S(1)}, bf16[1,112,768]{2,1,0:T(8,128)(2,1)S(1)}, u32[]{:S(2)}, u32[]{:S(2)}) collective-permute-start(bf16[1,112,768]{2,1,0:T(8,128)(2,1)S(1)} %pad_maximum_fusion.3.refs_0_), channel_id=1, source_target_pairs={{0,8},{4,12},{8,0},{12,4},{16,24},{20,28},{24,16},{28,20},{1,9},{5... | collective-permute-start | bytes 516104 | tf_op jit(solution)/shard_map/ppermute | solution.py:56
  8.2 19.1 %collective-permute-start.4 = (bf16[1,112,768]{2,1,0:T(8,128)(2,1)S(1)}, bf16[1,112,768]{2,1,0:T(8,128)(2,1)S(1)}, u32[]{:S(2)}, u32[]{:S(2)}) collective-permute-start(bf16[1,112,768]{2,1,0:T(8,128)(2,1)S(1)} %pad_maximum_fusion.3.refs_0_), channel_id=1, source_target_pairs={{0,16},{4,20},{8,24},{12,28},{16,0},{20,4},{24,8},{28,12},{1,17},{... | collective-permute-start | bytes 516104 | tf_op jit(solution)/shard_map/ppermute | solution.py:56
  14.4 11.1 %copy-start.25 = (f32[96,768]{1,0:T(8,128)S(1)}, f32[96,768]{1,0:T(8,128)}, u32[]{:S(2)}) copy-start(f32[96,768]{1,0:T(8,128)} %first.1) | copy-start | bytes 884740
  14.4 11.1 %copy-start.27 = (f32[96,768]{1,0:T(8,128)S(1)}, f32[96,768]{1,0:T(8,128)}, u32[]{:S(2)}) copy-start(f32[96,768]{1,0:T(8,128)} %second.1) | copy-start | bytes 884740
  15.9 10.5 %copy-start.48 = (bf16[1,96,768]{2,1,0:T(8,128)(2,1)S(1)}, bf16[1,96,768]{2,1,0:T(8,128)(2,1)}, u32[]{:S(2)}) copy-start(bf16[1,96,768]{2,1,0:T(8,128)(2,1)} %shard_map.450) | copy-start | bytes 442372
  15.9 5.4 %collective-permute-start.1 = (bf16[1,96,768]{2,1,0:T(8,128)(2,1)}, bf16[1,96,768]{2,1,0:T(8,128)(2,1)S(1)}, u32[]{:S(2)}, u32[]{:S(2)}) collective-permute-start(bf16[1,96,768]{2,1,0:T(8,128)(2,1)} %shard_map.450), channel_id=1, source_target_pairs={{0,4},{4,0},{8,12},{12,8},{16,20},{20,16},{24,28},{28,24},{1,5},{5... | collective-permute-start | bytes 442376 | tf_op jit(solution)/shard_map/ppermute | solution.py:56
  17.5 8.7 %collective-permute-start.2 = (bf16[1,96,768]{2,1,0:T(8,128)(2,1)}, bf16[1,96,768]{2,1,0:T(8,128)(2,1)S(1)}, u32[]{:S(2)}, u32[]{:S(2)}) collective-permute-start(bf16[1,96,768]{2,1,0:T(8,128)(2,1)} %shard_map.450), channel_id=1, source_target_pairs={{0,2},{1,3},{2,0},{3,1},{4,6},{5,7},{6,4},{7,5},{8,10},{9,11},{10,... | collective-permute-start | bytes 442376 | tf_op jit(solution)/shard_map/ppermute | solution.py:56
  21.2 5.1 %collective-permute-start.3 = (bf16[1,96,768]{2,1,0:T(8,128)(2,1)S(1)}, bf16[1,96,768]{2,1,0:T(8,128)(2,1)S(1)}, u32[]{:S(2)}, u32[]{:S(2)}) collective-permute-start(bf16[1,96,768]{2,1,0:T(8,128)(2,1)S(1)} %collective-permute-done.1), channel_id=1, source_target_pairs={{0,2},{1,3},{2,0},{3,1},{4,6},{5,7},{6,4},{7,5},{8,10},{9,11},{10,... | collective-permute-start | bytes 442376 | tf_op jit(solution)/shard_map/ppermute | solution.py:56
  28.4 21.1 %copy-start.12 = (bf16[4,1,112,768]{3,2,1,0:T(8,128)(2,1)}, bf16[4,1,112,768]{3,2,1,0:T(8,128)(2,1)S(1)}, u32[]{:S(2)}) copy-start(bf16[4,1,112,768]{3,2,1,0:T(8,128)(2,1)S(1)} %pad_maximum_fusion.1.refs_0_) | copy-start | bytes 2064388
  28.4 16.4 %collective-permute-start.6 = (bf16[4,1,112,768]{3,2,1,0:T(8,128)(2,1)S(1)}, bf16[4,1,112,768]{3,2,1,0:T(8,128)(2,1)}, u32[]{:S(2)}, u32[]{:S(2)}) collective-permute-start(bf16[4,1,112,768]{3,2,1,0:T(8,128)(2,1)S(1)} %pad_maximum_fusion.1.refs_0_), channel_id=1, source_target_pairs={{0,4},{4,0},{8,12},{12,8},{16,20},{20,16},{24,28},{28,24},{1,5},{5... | collective-permute-start | bytes 2064392 | tf_op jit(solution)/shard_map/ppermute | solution.py:56
  30.2 14.9 %collective-permute-start.7 = (bf16[4,1,112,768]{3,2,1,0:T(8,128)(2,1)S(1)}, bf16[4,1,112,768]{3,2,1,0:T(8,128)(2,1)}, u32[]{:S(2)}, u32[]{:S(2)}) collective-permute-start(bf16[4,1,112,768]{3,2,1,0:T(8,128)(2,1)S(1)} %pad_maximum_fusion.1.refs_0_), channel_id=1, source_target_pairs={{0,2},{1,3},{2,0},{3,1},{4,6},{5,7},{6,4},{7,5},{8,10},{9,11},{10,... | collective-permute-start | bytes 2064392 | tf_op jit(solution)/shard_map/ppermute | solution.py:56
  31.7 13.1 %collective-permute-start.8 = (bf16[2,96,768]{2,1,0:T(8,128)(2,1)}, bf16[2,96,768]{2,1,0:T(8,128)(2,1)S(1)}, u32[]{:S(2)}, u32[]{:S(2)}) collective-permute-start(bf16[2,96,768]{2,1,0:T(8,128)(2,1)} %shard_map.452.refs_0_), channel_id=1, source_target_pairs={{0,16},{4,20},{8,24},{12,28},{16,0},{20,4},{24,8},{28,12},{1,17},{... | collective-permute-start | bytes 884744 | tf_op jit(solution)/shard_map/ppermute | solution.py:56
  33.8 11.1 %collective-permute-start.9 = (bf16[2,96,768]{2,1,0:T(8,128)(2,1)}, bf16[2,96,768]{2,1,0:T(8,128)(2,1)S(1)}, u32[]{:S(2)}, u32[]{:S(2)}) collective-permute-start(bf16[2,96,768]{2,1,0:T(8,128)(2,1)} %shard_map.452.refs_0_), channel_id=1, source_target_pairs={{0,8},{4,12},{8,0},{12,4},{16,24},{20,28},{24,16},{28,20},{1,9},{5... | collective-permute-start | bytes 884744 | tf_op jit(solution)/shard_map/ppermute | solution.py:56
  44.7 12.1 %copy-start.14 = (bf16[2,96,768]{2,1,0:T(8,128)(2,1)}, bf16[2,96,768]{2,1,0:T(8,128)(2,1)S(1)}, u32[]{:S(2)}) copy-start(bf16[2,96,768]{2,1,0:T(8,128)(2,1)S(1)} %collective-permute-done.8.refs_0_.refs_1_) | copy-start | bytes 884740
  44.9 11.9 %copy-start.15 = (bf16[2,96,768]{2,1,0:T(8,128)(2,1)}, bf16[2,96,768]{2,1,0:T(8,128)(2,1)S(1)}, u32[]{:S(2)}) copy-start(bf16[2,96,768]{2,1,0:T(8,128)(2,1)S(1)} %collective-permute-done.9.refs_1_.refs_2_) | copy-start | bytes 884740
  46.2 8.7 %collective-permute-start.10 = (bf16[2,1,112,768]{3,2,1,0:T(8,128)(2,1)S(1)}, bf16[2,1,112,768]{3,2,1,0:T(8,128)(2,1)}, u32[]{:S(2)}, u32[]{:S(2)}) collective-permute-start(bf16[2,1,112,768]{3,2,1,0:T(8,128)(2,1)S(1)} %get-tuple-element.83), channel_id=1, source_target_pairs={{0,2},{1,3},{2,0},{3,1},{4,6},{5,7},{6,4},{7,5},{8,10},{9,11},{10,... | collective-permute-start | bytes 1032200 | tf_op jit(solution)/shard_map/ppermute | solution.py:56
  47.3 8.7 %collective-permute-start.11 = (bf16[2,1,112,768]{3,2,1,0:T(8,128)(2,1)S(1)}, bf16[2,1,112,768]{3,2,1,0:T(8,128)(2,1)S(1)}, u32[]{:S(2)}, u32[]{:S(2)}) collective-permute-start(bf16[2,1,112,768]{3,2,1,0:T(8,128)(2,1)S(1)} %get-tuple-element.84), channel_id=1, source_target_pairs={{0,4},{4,0},{8,12},{12,8},{16,20},{20,16},{24,28},{28,24},{1,5},{5... | collective-permute-start | bytes 1032200 | tf_op jit(solution)/shard_map/ppermute | solution.py:56
  48.3 8.5 %collective-permute-start.19 = (bf16[2,96,768]{2,1,0:T(8,128)(2,1)S(1)}, bf16[2,96,768]{2,1,0:T(8,128)(2,1)S(1)}, u32[]{:S(2)}, u32[]{:S(2)}) collective-permute-start(bf16[2,96,768]{2,1,0:T(8,128)(2,1)S(1)} %collective-permute-done.8.refs_0_.refs_1_), channel_id=1, source_target_pairs={{0,8},{4,12},{8,0},{12,4},{16,24},{20,28},{24,16},{28,20},{1,9},{5... | collective-permute-start | bytes 884744 | tf_op jit(solution)/shard_map/ppermute | solution.py:56
  49.5 11.4 %collective-permute-start.12 = (bf16[4,1,112,768]{3,2,1,0:T(8,128)(2,1)S(1)}, bf16[4,1,112,768]{3,2,1,0:T(8,128)(2,1)}, u32[]{:S(2)}, u32[]{:S(2)}) collective-permute-start(bf16[4,1,112,768]{3,2,1,0:T(8,128)(2,1)S(1)} %pad_maximum_fusion.1.refs_0_), channel_id=1, source_target_pairs={{0,1},{1,0},{2,3},{3,2},{4,5},{5,4},{6,7},{7,6},{8,9},{9,8},{10,11... | collective-permute-start | bytes 2064392 | tf_op jit(solution)/shard_map/ppermute | solution.py:56
  49.5 11.4 %collective-permute-start.13 = (bf16[4,1,112,768]{3,2,1,0:T(8,128)(2,1)}, bf16[4,1,112,768]{3,2,1,0:T(8,128)(2,1)}, u32[]{:S(2)}, u32[]{:S(2)}) collective-permute-start(bf16[4,1,112,768]{3,2,1,0:T(8,128)(2,1)} %collective-permute-done.6.from_y.refs_1_), channel_id=1, source_target_pairs={{0,1},{1,0},{2,3},{3,2},{4,5},{5,4},{6,7},{7,6},{8,9},{9,8},{10,11... | collective-permute-start | bytes 2064392 | tf_op jit(solution)/shard_map/ppermute | solution.py:56
  54.9 6.6 %collective-permute-start.14 = (bf16[4,1,112,768]{3,2,1,0:T(8,128)(2,1)}, bf16[4,1,112,768]{3,2,1,0:T(8,128)(2,1)}, u32[]{:S(2)}, u32[]{:S(2)}) collective-permute-start(bf16[4,1,112,768]{3,2,1,0:T(8,128)(2,1)} %collective-permute-done.7.from_x.refs_2_), channel_id=1, source_target_pairs={{0,1},{1,0},{2,3},{3,2},{4,5},{5,4},{6,7},{7,6},{8,9},{9,8},{10,11... | collective-permute-start | bytes 2064392 | tf_op jit(solution)/shard_map/ppermute | solution.py:56
  59.1 30.2 %collective-permute-start.20 = (bf16[4,2,96,768]{3,2,1,0:T(8,128)(2,1)}, bf16[4,2,96,768]{3,2,1,0:T(8,128)(2,1)}, u32[]{:S(2)}, u32[]{:S(2)}) collective-permute-start(bf16[4,2,96,768]{3,2,1,0:T(8,128)(2,1)} %pad_maximum_fusion.refs_4_.refs_8_), channel_id=1, source_target_pairs={{0,4},{4,0},{8,12},{12,8},{16,20},{20,16},{24,28},{28,24},{1,5},{5... | collective-permute-start | bytes 3538952 | tf_op jit(solution)/shard_map/ppermute | solution.py:56
  59.4 29.8 %collective-permute-start.21 = (bf16[4,2,96,768]{3,2,1,0:T(8,128)(2,1)}, bf16[4,2,96,768]{3,2,1,0:T(8,128)(2,1)S(1)}, u32[]{:S(2)}, u32[]{:S(2)}) collective-permute-start(bf16[4,2,96,768]{3,2,1,0:T(8,128)(2,1)} %pad_maximum_fusion.refs_4_.refs_8_), channel_id=1, source_target_pairs={{0,2},{1,3},{2,0},{3,1},{4,6},{5,7},{6,4},{7,5},{8,10},{9,11},{10,... | collective-permute-start | bytes 3538952 | tf_op jit(solution)/shard_map/ppermute | solution.py:56
  60.9 3.8 %collective-permute-start.15 = (bf16[2,1,112,768]{3,2,1,0:T(8,128)(2,1)}, bf16[2,1,112,768]{3,2,1,0:T(8,128)(2,1)}, u32[]{:S(2)}, u32[]{:S(2)}) collective-permute-start(bf16[2,1,112,768]{3,2,1,0:T(8,128)(2,1)} %collective-permute-done.10.refs_3_.refs_1_), channel_id=1, source_target_pairs={{0,1},{1,0},{2,3},{3,2},{4,5},{5,4},{6,7},{7,6},{8,9},{9,8},{10,11... | collective-permute-start | bytes 1032200 | tf_op jit(solution)/shard_map/ppermute | solution.py:56
  60.9 28.3 %collective-permute-start.22 = (bf16[1,4,96,768]{3,2,1,0:T(8,128)(2,1)}, bf16[1,4,96,768]{3,2,1,0:T(8,128)(2,1)S(1)}, u32[]{:S(2)}, u32[]{:S(2)}) collective-permute-start(bf16[1,4,96,768]{3,2,1,0:T(8,128)(2,1)} %bitcast.75), channel_id=1, source_target_pairs={{0,8},{4,12},{8,0},{12,4},{16,24},{20,28},{24,16},{28,20},{1,9},{5... | collective-permute-start | bytes 1769480 | tf_op jit(solution)/shard_map/ppermute | solution.py:56
  61.5 31.6 %collective-permute-start.25 = (bf16[1,4,96,768]{3,2,1,0:T(8,128)(2,1)}, bf16[1,4,96,768]{3,2,1,0:T(8,128)(2,1)S(1)}, u32[]{:S(2)}, u32[]{:S(2)}) collective-permute-start(bf16[1,4,96,768]{3,2,1,0:T(8,128)(2,1)} %bitcast.76), channel_id=1, source_target_pairs={{0,16},{4,20},{8,24},{12,28},{16,0},{20,4},{24,8},{28,12},{1,17},{... | collective-permute-start | bytes 1769480 | tf_op jit(solution)/shard_map/ppermute | solution.py:56
  64.8 1.7 collective-permute-start.16
  90.8 14.9 %collective-permute-start.23 = (bf16[2,2,96,768]{3,2,1,0:T(8,128)(2,1)S(1)}, bf16[2,2,96,768]{3,2,1,0:T(8,128)(2,1)S(1)}, u32[]{:S(2)}, u32[]{:S(2)}) collective-permute-start(bf16[2,2,96,768]{3,2,1,0:T(8,128)(2,1)S(1)} %get-tuple-element.88), channel_id=1, source_target_pairs={{0,2},{1,3},{2,0},{3,1},{4,6},{5,7},{6,4},{7,5},{8,10},{9,11},{10,... | collective-permute-start | bytes 1769480 | tf_op jit(solution)/shard_map/ppermute | solution.py:56
  91.4 14.6 %collective-permute-start.24 = (bf16[2,2,96,768]{3,2,1,0:T(8,128)(2,1)S(1)}, bf16[2,2,96,768]{3,2,1,0:T(8,128)(2,1)S(1)}, u32[]{:S(2)}, u32[]{:S(2)}) collective-permute-start(bf16[2,2,96,768]{3,2,1,0:T(8,128)(2,1)S(1)} %get-tuple-element.89), channel_id=1, source_target_pairs={{0,4},{4,0},{8,12},{12,8},{16,20},{20,16},{24,28},{28,24},{1,5},{5... | collective-permute-start | bytes 1769480 | tf_op jit(solution)/shard_map/ppermute | solution.py:56
  93.1 23.4 %collective-permute-start.26 = (bf16[1,4,96,768]{3,2,1,0:T(8,128)(2,1)S(1)}, bf16[1,4,96,768]{3,2,1,0:T(8,128)(2,1)S(1)}, u32[]{:S(2)}, u32[]{:S(2)}) collective-permute-start(bf16[1,4,96,768]{3,2,1,0:T(8,128)(2,1)S(1)} %collective-permute-done.25.refs_9_.refs_1_.refs_5_.refs_13_.refs_11_.refs_15_), channel_id=1, source_target_pairs={{0,8},{4,12},{8,0},{12,4},{16,24},{20,28},{24,16},{28,20},{1,9},{5... | collective-permute-start | bytes 1769480 | tf_op jit(solution)/shard_map/ppermute | solution.py:56
  93.1 1.7 collective-permute-start.17
  93.1 23.4 %copy-start = (bf16[4,96,768]{2,1,0:T(8,128)(2,1)S(1)}, bf16[4,96,768]{2,1,0:T(8,128)(2,1)}, u32[]{:S(2)}) copy-start(bf16[4,96,768]{2,1,0:T(8,128)(2,1)} %shard_map.456) | copy-start | bytes 1769476
  93.2 2.3 collective-permute-start.18
  125.3 3.8 %collective-permute-start.27 = (f32[512,768]{1,0:T(8,128)}, f32[512,768]{1,0:T(8,128)}, u32[]{:S(2)}, u32[]{:S(2)}) collective-permute-start(f32[512,768]{1,0:T(8,128)} %get-tuple-element.91), channel_id=1, source_target_pairs={{0,1},{1,0},{2,3},{3,2},{4,5},{5,4},{6,7},{7,6},{8,9},{9,8},{10,11... | collective-permute-start | bytes 4718600 | tf_op jit(solution)/shard_map/ppermute | solution.py:56
  125.4 11.9 %collective-permute-start.31 = (bf16[128,768]{1,0:T(8,128)(2,1)}, bf16[128,768]{1,0:T(8,128)(2,1)S(1)}, u32[]{:S(2)}, u32[]{:S(2)}) collective-permute-start(bf16[128,768]{1,0:T(8,128)(2,1)} %shard_map.461.refs_4_), channel_id=1, source_target_pairs={{0,2},{1,3},{2,0},{3,1},{4,6},{5,7},{6,4},{7,5},{8,10},{9,11},{10,... | collective-permute-start | bytes 589832 | tf_op jit(solution)/shard_map/ppermute | solution.py:56
  131.9 12.2 %copy-start.42 = (s32[8]{0:T(128)S(1)}, s32[8]{0:T(128)}, u32[]{:S(2)}) copy-start(s32[8]{0:T(128)} %broadcast_multiply_fusion.refs_3_.rows.refs_16_) | copy-start | bytes 100
  135.8 6.9 %collective-permute-start.28 = (bf16[128,768]{1,0:T(8,128)(2,1)S(1)}, bf16[128,768]{1,0:T(8,128)(2,1)S(1)}, u32[]{:S(2)}, u32[]{:S(2)}) collective-permute-start(bf16[128,768]{1,0:T(8,128)(2,1)S(1)} %get-tuple-element.95.refs_0_), channel_id=1, source_target_pairs={{0,2},{1,3},{2,0},{3,1},{4,6},{5,7},{6,4},{7,5},{8,10},{9,11},{10,... | collective-permute-start | bytes 589832 | tf_op jit(solution)/shard_map/ppermute | solution.py:56
  137.2 5.5 %collective-permute-start.32 = (bf16[128,768]{1,0:T(8,128)(2,1)S(1)}, bf16[128,768]{1,0:T(8,128)(2,1)S(1)}, u32[]{:S(2)}, u32[]{:S(2)}) collective-permute-start(bf16[128,768]{1,0:T(8,128)(2,1)S(1)} %copy-done.32), channel_id=1, source_target_pairs={{0,1},{1,0},{2,3},{3,2},{4,5},{5,4},{6,7},{7,6},{8,9},{9,8},{10,11... | collective-permute-start | bytes 589832 | tf_op jit(solution)/shard_map/ppermute | solution.py:56
  137.2 5.5 %collective-permute-start.33 = (bf16[128,768]{1,0:T(8,128)(2,1)S(1)}, bf16[128,768]{1,0:T(8,128)(2,1)S(1)}, u32[]{:S(2)}, u32[]{:S(2)}) collective-permute-start(bf16[128,768]{1,0:T(8,128)(2,1)S(1)} %collective-permute-done.31.refs_5_), channel_id=1, source_target_pairs={{0,1},{1,0},{2,3},{3,2},{4,5},{5,4},{6,7},{7,6},{8,9},{9,8},{10,11... | collective-permute-start | bytes 589832 | tf_op jit(solution)/shard_map/ppermute | solution.py:56
  137.8 5.0 %collective-permute-start.29 = (bf16[128,768]{1,0:T(8,128)(2,1)S(1)}, bf16[128,768]{1,0:T(8,128)(2,1)S(1)}, u32[]{:S(2)}, u32[]{:S(2)}) collective-permute-start(bf16[128,768]{1,0:T(8,128)(2,1)S(1)} %get-tuple-element.95.refs_0_), channel_id=1, source_target_pairs={{0,1},{1,0},{2,3},{3,2},{4,5},{5,4},{6,7},{7,6},{8,9},{9,8},{10,11... | collective-permute-start | bytes 589832 | tf_op jit(solution)/shard_map/ppermute | solution.py:56
  142.7 1.4 collective-permute-start.30
  150.7 5.5 %collective-permute-start.34 = (f32[2,128,768]{2,1,0:T(8,128)S(1)}, f32[2,128,768]{2,1,0:T(8,128)S(1)}, u32[]{:S(2)}, u32[]{:S(2)}) collective-permute-start(f32[2,128,768]{2,1,0:T(8,128)S(1)} %get-tuple-element.98), channel_id=1, source_target_pairs={{0,1},{1,0},{2,3},{3,2},{4,5},{5,4},{6,7},{7,6},{8,9},{9,8},{10,11... | collective-permute-start | bytes 2359304 | tf_op jit(solution)/shard_map/ppermute | solution.py:56
  153.0 28.9 %collective-permute-start.36 = (bf16[4,2,96,768]{3,2,1,0:T(8,128)(2,1)S(1)}, bf16[4,2,96,768]{3,2,1,0:T(8,128)(2,1)S(1)}, u32[]{:S(2)}, u32[]{:S(2)}) collective-permute-start(bf16[4,2,96,768]{3,2,1,0:T(8,128)(2,1)S(1)} %get-tuple-element.114), channel_id=1, source_target_pairs={{0,4},{4,0},{8,12},{12,8},{16,20},{20,16},{24,28},{28,24},{1,5},{5... | collective-permute-start | bytes 3538952 | tf_op jit(solution)/shard_map/ppermute | solution.py:56
  154.8 8.6 %copy-start.38 = (bf16[128,768]{1,0:T(8,128)(2,1)S(1)}, bf16[128,768]{1,0:T(8,128)(2,1)}, u32[]{:S(2)}) copy-start(bf16[128,768]{1,0:T(8,128)(2,1)} %copy-done.37) | copy-start | bytes 589828
  156.5 6.9 %collective-permute-start.35 = (bf16[128,768]{1,0:T(8,128)(2,1)S(1)}, bf16[128,768]{1,0:T(8,128)(2,1)S(1)}, u32[]{:S(2)}, u32[]{:S(2)}) collective-permute-start(bf16[128,768]{1,0:T(8,128)(2,1)S(1)} %fusion.6), channel_id=1, source_target_pairs={{0,2},{1,3},{2,0},{3,1},{4,6},{5,7},{6,4},{7,5},{8,10},{9,11},{10,... | collective-permute-start | bytes 589832 | tf_op jit(solution)/shard_map/ppermute | solution.py:56
  174.5 2.1 collective-permute-start.37
  174.5 3.1 %collective-permute-start.38 = (bf16[4,112,768]{2,1,0:T(8,128)(2,1)S(1)}, bf16[4,112,768]{2,1,0:T(8,128)(2,1)S(1)}, u32[]{:S(2)}, u32[]{:S(2)}) collective-permute-start(bf16[4,112,768]{2,1,0:T(8,128)(2,1)S(1)} %get-tuple-element.117), channel_id=1, source_target_pairs={{0,1},{1,0},{2,3},{3,2},{4,5},{5,4},{6,7},{7,6},{8,9},{9,8},{10,11... | collective-permute-start | bytes 2064392 | tf_op jit(solution)/shard_map/ppermute | solution.py:56
  175.0 3.6 %collective-permute-start.39 = (bf16[4,112,768]{2,1,0:T(8,128)(2,1)S(1)}, bf16[4,112,768]{2,1,0:T(8,128)(2,1)S(1)}, u32[]{:S(2)}, u32[]{:S(2)}) collective-permute-start(bf16[4,112,768]{2,1,0:T(8,128)(2,1)S(1)} %get-tuple-element.118), channel_id=1, source_target_pairs={{0,1},{1,0},{2,3},{3,2},{4,5},{5,4},{6,7},{7,6},{8,9},{9,8},{10,11... | collective-permute-start | bytes 2064392 | tf_op jit(solution)/shard_map/ppermute | solution.py:56
  175.0 4.6 %collective-permute-start.40 = (bf16[4,112,768]{2,1,0:T(8,128)(2,1)S(1)}, bf16[4,112,768]{2,1,0:T(8,128)(2,1)S(1)}, u32[]{:S(2)}, u32[]{:S(2)}) collective-permute-start(bf16[4,112,768]{2,1,0:T(8,128)(2,1)S(1)} %get-tuple-element.119), channel_id=1, source_target_pairs={{0,1},{1,0},{2,3},{3,2},{4,5},{5,4},{6,7},{7,6},{8,9},{9,8},{10,11... | collective-permute-start | bytes 2064392 | tf_op jit(solution)/shard_map/ppermute | solution.py:56
  176.7 17.9 %collective-permute-start.42 = (bf16[4,1,96,768]{3,2,1,0:T(8,128)(2,1)S(1)}, bf16[4,1,96,768]{3,2,1,0:T(8,128)(2,1)S(1)}, u32[]{:S(2)}, u32[]{:S(2)}) collective-permute-start(bf16[4,1,96,768]{3,2,1,0:T(8,128)(2,1)S(1)} %get-tuple-element.110._), channel_id=1, source_target_pairs={{0,4},{4,0},{8,12},{12,8},{16,20},{20,16},{24,28},{28,24},{1,5},{5... | collective-permute-start | bytes 1769480 | tf_op jit(solution)/shard_map/ppermute | solution.py:56
  179.8 14.8 %collective-permute-start.43 = (bf16[2,112,768]{2,1,0:T(8,128)(2,1)S(1)}, bf16[2,112,768]{2,1,0:T(8,128)(2,1)S(1)}, u32[]{:S(2)}, u32[]{:S(2)}) collective-permute-start(bf16[2,112,768]{2,1,0:T(8,128)(2,1)S(1)} %get-tuple-element.120.refs_0_), channel_id=1, source_target_pairs={{0,2},{1,3},{2,0},{3,1},{4,6},{5,7},{6,4},{7,5},{8,10},{9,11},{10,... | collective-permute-start | bytes 1032200 | tf_op jit(solution)/shard_map/ppermute | solution.py:56
  180.4 21.0 %collective-permute-start.44 = (bf16[2,112,768]{2,1,0:T(8,128)(2,1)S(1)}, bf16[2,112,768]{2,1,0:T(8,128)(2,1)S(1)}, u32[]{:S(2)}, u32[]{:S(2)}) collective-permute-start(bf16[2,112,768]{2,1,0:T(8,128)(2,1)S(1)} %get-tuple-element.126), channel_id=1, source_target_pairs={{0,4},{4,0},{8,12},{12,8},{16,20},{20,16},{24,28},{28,24},{1,5},{5... | collective-permute-start | bytes 1032200 | tf_op jit(solution)/shard_map/ppermute | solution.py:56
  182.2 22.1 %collective-permute-start.41 = (bf16[2,2,96,768]{3,2,1,0:T(8,128)(2,1)S(1)}, bf16[2,2,96,768]{3,2,1,0:T(8,128)(2,1)S(1)}, u32[]{:S(2)}, u32[]{:S(2)}) collective-permute-start(bf16[2,2,96,768]{3,2,1,0:T(8,128)(2,1)S(1)} %get-tuple-element.122), channel_id=1, source_target_pairs={{0,8},{4,12},{8,0},{12,4},{16,24},{20,28},{24,16},{28,20},{1,9},{5... | collective-permute-start | bytes 1769480 | tf_op jit(solution)/shard_map/ppermute | solution.py:56
  201.8 17.4 %collective-permute-start.45 = (bf16[4,112,768]{2,1,0:T(8,128)(2,1)S(1)}, bf16[4,112,768]{2,1,0:T(8,128)(2,1)S(1)}, u32[]{:S(2)}, u32[]{:S(2)}) collective-permute-start(bf16[4,112,768]{2,1,0:T(8,128)(2,1)S(1)} %get-tuple-element.127.refs_0_), channel_id=1, source_target_pairs={{0,2},{1,3},{2,0},{3,1},{4,6},{5,7},{6,4},{7,5},{8,10},{9,11},{10,... | collective-permute-start | bytes 2064392 | tf_op jit(solution)/shard_map/ppermute | solution.py:56
  203.3 16.6 %collective-permute-start.46 = (bf16[4,112,768]{2,1,0:T(8,128)(2,1)S(1)}, bf16[4,112,768]{2,1,0:T(8,128)(2,1)S(1)}, u32[]{:S(2)}, u32[]{:S(2)}) collective-permute-start(bf16[4,112,768]{2,1,0:T(8,128)(2,1)S(1)} %get-tuple-element.131), channel_id=1, source_target_pairs={{0,4},{4,0},{8,12},{12,8},{16,20},{20,16},{24,28},{28,24},{1,5},{5... | collective-permute-start | bytes 2064392 | tf_op jit(solution)/shard_map/ppermute | solution.py:56
  204.2 13.1 %collective-permute-start.51 = (bf16[2,1,96,768]{3,2,1,0:T(8,128)(2,1)S(1)}, bf16[2,1,96,768]{3,2,1,0:T(8,128)(2,1)S(1)}, u32[]{:S(2)}, u32[]{:S(2)}) collective-permute-start(bf16[2,1,96,768]{3,2,1,0:T(8,128)(2,1)S(1)} %get-tuple-element.128.refs_0_), channel_id=1, source_target_pairs={{0,8},{4,12},{8,0},{12,4},{16,24},{20,28},{24,16},{28,20},{1,9},{5... | collective-permute-start | bytes 884744 | tf_op jit(solution)/shard_map/ppermute | solution.py:56
  204.5 21.1 %collective-permute-start.50 = (bf16[2,96,768]{2,1,0:T(8,128)(2,1)S(1)}, bf16[2,96,768]{2,1,0:T(8,128)(2,1)S(1)}, u32[]{:S(2)}, u32[]{:S(2)}) collective-permute-start(bf16[2,96,768]{2,1,0:T(8,128)(2,1)S(1)} %bitcast.90), channel_id=1, source_target_pairs={{0,16},{4,20},{8,24},{12,28},{16,0},{20,4},{24,8},{28,12},{1,17},{... | collective-permute-start | bytes 884744 | tf_op jit(solution)/shard_map/ppermute | solution.py:56
  218.8 15.9 %collective-permute-start.52 = (bf16[1,96,768]{2,1,0:T(8,128)(2,1)S(1)}, bf16[1,96,768]{2,1,0:T(8,128)(2,1)S(1)}, u32[]{:S(2)}, u32[]{:S(2)}) collective-permute-start(bf16[1,96,768]{2,1,0:T(8,128)(2,1)S(1)} %bitcast.91), channel_id=1, source_target_pairs={{0,16},{4,20},{8,24},{12,28},{16,0},{20,4},{24,8},{28,12},{1,17},{... | collective-permute-start | bytes 442376 | tf_op jit(solution)/shard_map/ppermute | solution.py:56
  221.2 16.3 %collective-permute-start.49 = (bf16[112,768]{1,0:T(8,128)(2,1)S(1)}, bf16[112,768]{1,0:T(8,128)(2,1)S(1)}, u32[]{:S(2)}, u32[]{:S(2)}) collective-permute-start(bf16[112,768]{1,0:T(8,128)(2,1)S(1)} %get-tuple-element.135), channel_id=1, source_target_pairs={{0,24},{4,28},{8,16},{12,20},{16,8},{20,12},{24,0},{28,4},{1,25},{... | collective-permute-start | bytes 516104 | tf_op jit(solution)/shard_map/ppermute | solution.py:56
  223.4 18.4 %collective-permute-start.48 = (bf16[112,768]{1,0:T(8,128)(2,1)S(1)}, bf16[112,768]{1,0:T(8,128)(2,1)S(1)}, u32[]{:S(2)}, u32[]{:S(2)}) collective-permute-start(bf16[112,768]{1,0:T(8,128)(2,1)S(1)} %get-tuple-element.134), channel_id=1, source_target_pairs={{0,16},{4,20},{8,24},{12,28},{16,0},{20,4},{24,8},{28,12},{1,17},{... | collective-permute-start | bytes 516104 | tf_op jit(solution)/shard_map/ppermute | solution.py:56
  224.2 17.6 %collective-permute-start.47 = (bf16[112,768]{1,0:T(8,128)(2,1)S(1)}, bf16[112,768]{1,0:T(8,128)(2,1)S(1)}, u32[]{:S(2)}, u32[]{:S(2)}) collective-permute-start(bf16[112,768]{1,0:T(8,128)(2,1)S(1)} %get-tuple-element.133), channel_id=1, source_target_pairs={{0,8},{4,12},{8,0},{12,4},{16,24},{20,28},{24,16},{28,20},{1,9},{5... | collective-permute-start | bytes 516104 | tf_op jit(solution)/shard_map/ppermute | solution.py:56
  (66 other events, 249.5 us)
where the time goes:
time: 250 us; the launch traced here: 245 us
  waiting for transfers between devices  87.6 us (35%)
  Pallas kernels  60.9 us (24%)
  starting transfers between devices  49.1 us (20%)
  local copies, waits for them, and re-layouts  26 us (10%)
  other arithmetic  17.4 us (7%)
  between operations  2.73 us (1%)
    ppermute x53, waiting for transfers between devices, flip(): return lax.ppermute(block, axis, [(i, i ^ bits) for i in range(size)])  87.6 us
    ppermute x53, starting transfers between devices, flip(): return lax.ppermute(block, axis, [(i, i ^ bits) for i in range(size)])  49.1 us
    unnamed x154, local copies, waits for them, and re-layouts  19.5 us
    pallas_call x1, Pallas kernels, first_part(): kernel_call(partial(first_kernel, [len(group) for group in groups], extra...  11.8 us
    pallas_call x1, Pallas kernels, attend_back(): kernel_call(partial(attend_kernel, extra), [like((count, width), jnp.floa...  11.1 us
    pallas_call x1, Pallas kernels, ffn_front(): kernel_call(partial(front_kernel, (len(near), len(far))), [like((2, 4 * q...  9.26 us
    pallas_call x1, Pallas kernels, ffn_down(): kernel_call(partial(down_kernel, [[lot for _, lot in group] for group in...  7.58 us
    sub x6, other arithmetic, adamw_step(): master - step_rate * (moment / fix_one / (jnp.sqrt(squares / fix_two) + a...  6.83 us
  transfers between devices with their start and end apart: 53, of which 28 were waited for; matrix products, arithmetic and copies ran while one was open for 8% of the time, Pallas kernels for 19%

commit v1 on v0

--- a/solution.py
+++ b/solution.py
@@ -871,6 +871,10 @@
         packed_z = [packed] + [flip(packed, "dp", 2 * k) for k in (2, 1, 3)]
         wide = cast_wide(gate_master, value_master, packed_z[2])
 
+        deep = after(deep, packed_z[2])
+        deep_y, deep_x = flip_y(deep), flip_x(deep)
+        replace_rows = after(replace_rows, deep_y)
+
     live_slots = jnp.arange(slot_count, dtype=jnp.int32)[None, :] < masked_counts[:, None]
     at_slot = masked_positions[:, :, None] == jnp.arange(length, dtype=jnp.int32)[None, None, :]
     place_bool = at_slot & live_slots[:, :, None]
@@ -888,14 +892,12 @@
     live = live_slots.astype(jnp.float32).reshape(slot_rows, 1)
     indices = [rows, places, columns, spots, positions, live]
     if small:
-        deep = after(deep, start_rows)
-        deep_y, deep_x = flip_y(deep), flip_x(deep)
         deep_parts = jnp.concatenate([deep, deep_y, deep_x, flip_x(deep_y)])
         packed_z[0] = after(packed_z[0], wide, deep_parts, *indices)
         wide_z = gather_z(after(wide, packed_z[1], packed_z[3]))
         packed_z = jnp.stack(packed_z)
         packed_y, packed_x = flip_y(packed_z), flip_x(packed_z)
-        first_half, second_half = split_halves(packed_y, packed_x, wide_z[1], wide_z[2])
+        first_half, second_half = split_halves(packed_y, packed_x, wide_z[1], wide_z[2], start_rows)
         packed_near = [packed_z, packed_y]
         packed_far = [packed_x, flip_x(first_half), flip_y(second_half)]
         wide_z[0] = after(wide_z[0], *packed_far[1:])

time: 250 us -> 249 us (level)
  waiting for transfers between devices: 87.6 us -> 82.6 us
  local copies, waits for them, and re-layouts: 26 us -> 30.5 us
    ppermute x53, waiting for transfers between devices: 87.6 us -> 82.6 us  [flip(): return lax.ppermute(block, axis, [(i, i ^ bits) for i in range(size)])]
    unnamed x154 -> x161, local copies, waits for them, and re-layouts: 19.5 us -> 23.3 us
  transfers between devices with their start and end apart: 53 -> 53, of which waited for: 28 -> 26; matrix products, arithmetic and copies ran while one was open for 8% -> 8% of each run, Pallas kernels for 19% -> 19%
where the time goes in v1:
time: 249 us; the launch traced here: 245 us
  waiting for transfers between devices  82.6 us (33%)
  Pallas kernels  61 us (24%)
  starting transfers between devices  48.9 us (20%)
  local copies, waits for them, and re-layouts  30.5 us (12%)
  other arithmetic  18.3 us (7%)
  between operations  2.8 us (1%)
    ppermute x53, waiting for transfers between devices, flip(): return lax.ppermute(block, axis, [(i, i ^ bits) for i in range(size)])  82.6 us
    ppermute x53, starting transfers between devices, flip(): return lax.ppermute(block, axis, [(i, i ^ bits) for i in range(size)])  48.9 us
    unnamed x161, local copies, waits for them, and re-layouts  23.3 us
    pallas_call x1, Pallas kernels, first_part(): kernel_call(partial(first_kernel, [len(group) for group in groups], extra...  11.8 us
    pallas_call x1, Pallas kernels, attend_back(): kernel_call(partial(attend_kernel, extra), [like((count, width), jnp.floa...  11.1 us
    pallas_call x1, Pallas kernels, ffn_front(): kernel_call(partial(front_kernel, (len(near), len(far))), [like((2, 4 * q...  9.26 us
    pallas_call x1, Pallas kernels, ffn_down(): kernel_call(partial(down_kernel, [[lot for _, lot in group] for group in...  7.59 us
    sub x6, other arithmetic, adamw_step(): master - step_rate * (moment / fix_one / (jnp.sqrt(squares / fix_two) + a...  6.83 us
  transfers between devices with their start and end apart: 53, of which 26 were waited for; matrix products, arithmetic and copies ran while one was open for 8% of the time, Pallas kernels for 19%

profile of v1, /device:TPU:0, one launch (start us, length us, event | category | flops | bytes accessed | tf_op | source)
XLA Modules:
  0.0 244.6 jit_solution(3317027658614543164)
XLA Ops:
  0.7 1.3 copy.78.refs_0_
  4.3 3.1 %collective-permute-start = (bf16[1,112,768]{2,1,0:T(8,128)(2,1)S(1)}, bf16[1,112,768]{2,1,0:T(8,128)(2,1)S(1)}, u32[]{:S(2)}, u32[]{:S(2)}) collective-permute-start(bf16[1,112,768]{2,1,0:T(8,128)(2,1)S(1)} %pad_maximum_fusion.3.refs_0_), channel_id=1, source_target_pairs={{0,8},{4,12},{8,0},{12,4},{16,24},{20,28},{24,16},{28,20},{1,9},{5... | collective-permute-start | bytes 516104 | tf_op jit(solution)/shard_map/ppermute | solution.py:56
  7.4 2.5 %collective-permute-start.5 = (bf16[1,112,768]{2,1,0:T(8,128)(2,1)S(1)}, bf16[1,112,768]{2,1,0:T(8,128)(2,1)S(1)}, u32[]{:S(2)}, u32[]{:S(2)}) collective-permute-start(bf16[1,112,768]{2,1,0:T(8,128)(2,1)S(1)} %pad_maximum_fusion.3.refs_0_), channel_id=1, source_target_pairs={{0,24},{4,28},{8,16},{12,20},{16,8},{20,12},{24,0},{28,4},{1,25},{... | collective-permute-start | bytes 516104 | tf_op jit(solution)/shard_map/ppermute | solution.py:56
  12.9 1.5 collective-permute-start.1
  15.0 1.6 collective-permute-start.2
  16.6 1.6 collective-permute-done.1.refs_1_
  18.2 1.5 collective-permute-start.3
  24.8 1.8 pad_maximum_fusion.2.refs_2_.refs_0_
  27.9 1.6 collective-permute-start.6
  30.0 3.6 %collective-permute-start.8 = (bf16[2,96,768]{2,1,0:T(8,128)(2,1)}, bf16[2,96,768]{2,1,0:T(8,128)(2,1)S(1)}, u32[]{:S(2)}, u32[]{:S(2)}) collective-permute-start(bf16[2,96,768]{2,1,0:T(8,128)(2,1)} %shard_map.453.refs_0_), channel_id=1, source_target_pairs={{0,16},{4,20},{8,24},{12,28},{16,0},{20,4},{24,8},{28,12},{1,17},{... | collective-permute-start | bytes 884744 | tf_op jit(solution)/shard_map/ppermute | solution.py:56
  33.6 3.1 %collective-permute-start.9 = (bf16[2,96,768]{2,1,0:T(8,128)(2,1)}, bf16[2,96,768]{2,1,0:T(8,128)(2,1)S(1)}, u32[]{:S(2)}, u32[]{:S(2)}) collective-permute-start(bf16[2,96,768]{2,1,0:T(8,128)(2,1)} %shard_map.453.refs_0_), channel_id=1, source_target_pairs={{0,8},{4,12},{8,0},{12,4},{16,24},{20,28},{24,16},{28,20},{1,9},{5... | collective-permute-start | bytes 884744 | tf_op jit(solution)/shard_map/ppermute | solution.py:56
  36.7 4.6 %gather_fusion = bf16[128,768]{1,0:T(8,128)(2,1)S(1)} fusion(bf16[4096,768]{1,0:T(8,128)(2,1)} %param.27, s32[1024]{0:T(1024)S(1)} %pad_clamp_fusion), kind=kCustom, calls=%fused_computation | custom fusion | bytes 393728 | tf_op jit(solution)/shard_map/jit(_take)/gather | solution.py:881
  41.8 2.5 %collective-permute-done.8.refs_0_.refs_1_ = bf16[2,96,768]{2,1,0:T(8,128)(2,1)S(1)} collective-permute-done((bf16[2,96,768]{2,1,0:T(8,128)(2,1)}, bf16[2,96,768]{2,1,0:T(8,128)(2,1)S(1)}, u32[]{:S(2)}, u32[]{:S(2)}) %collective-permute-start.8) | collective-permute-done | bytes 294944 | tf_op jit(solution)/shard_map/ppermute | solution.py:56
  44.5 1.2 shard_map.454
  47.1 1.4 collective-permute-start.19
  49.1 6.0 %collective-permute-done.10.refs_3_.refs_1_ = bf16[2,1,112,768]{3,2,1,0:T(8,128)(2,1)} collective-permute-done((bf16[2,1,112,768]{3,2,1,0:T(8,128)(2,1)S(1)}, bf16[2,1,112,768]{3,2,1,0:T(8,128)(2,1)}, u32[]{:S(2)}, u32[]{:S(2)}) %collective-permute-start.10) | collective-permute-done | bytes 344096 | tf_op jit(solution)/shard_map/ppermute | solution.py:56
  55.8 2.2 pad_maximum_fusion.refs_4_.refs_8_
  58.7 1.6 collective-permute-start.21
  60.4 2.5 %collective-permute-start.25 = (bf16[1,4,96,768]{3,2,1,0:T(8,128)(2,1)}, bf16[1,4,96,768]{3,2,1,0:T(8,128)(2,1)S(1)}, u32[]{:S(2)}, u32[]{:S(2)}) collective-permute-start(bf16[1,4,96,768]{3,2,1,0:T(8,128)(2,1)} %bitcast.76), channel_id=1, source_target_pairs={{0,16},{4,20},{8,24},{12,28},{16,0},{20,4},{24,8},{28,12},{1,17},{... | collective-permute-start | bytes 1769480 | tf_op jit(solution)/shard_map/ppermute | solution.py:56
  62.9 1.6 collective-permute-done.16.refs_9_
  67.6 11.8 %shard_map.455 = (bf16[768,2304]{1,0:T(8,128)(2,1)S(1)}, bf16[768,768]{1,0:T(8,128)(2,1)S(1)}, bf16[512,2304]{1,0:T(8,128)(2,1)S(1)}, f32[512,768]{1,0:T(8,128)S...) custom-call(s32[4]{0:T(128)S(1)} %copy-done.45, ...), custom_call_target="tpu_custom_call" | custom-call | tf_op jit(solution)/shard_map/pallas_call | solution.py:300
  79.4 1.8 copy-done.7
  81.2 1.4 copy-done.15
  84.9 3.3 %collective-permute-done.22.refs_1_.refs_2_.refs_6_.refs_10_.refs_14_.refs_12_.refs_16_ = bf16[1,4,96,768]{3,2,1,0:T(8,128)(2,1)S(1)} collective-permute-done((bf16[1,4,96,768]{3,2,1,0:T(8,128)(2,1)}, bf16[1,4,96,768]{3,2,1,0:T(8,128)(2,1)S(1)}, u32[]{:S(2)}, u32[]{:S(2)}) %collective-permute-start.22) | collective-permute-done | bytes 589856 | tf_op jit(solution)/shard_map/ppermute | solution.py:56
  88.2 1.5 shard_map.458
  90.7 1.3 collective-permute-start.24
  92.5 1.2 collective-permute-done.17.refs_2_
  94.3 10.4 %collective-permute-done.23.refs_7_ = bf16[2,2,96,768]{3,2,1,0:T(8,128)(2,1)S(1)} collective-permute-done((bf16[2,2,96,768]{3,2,1,0:T(8,128)(2,1)S(1)}, bf16[2,2,96,768]{3,2,1,0:T(8,128)(2,1)S(1)}, u32[]{:S(2)}, u32[]{:S(2)}) %collective-permute-start.23) | collective-permute-done | bytes 589856 | tf_op jit(solution)/shard_map/ppermute | solution.py:56
  105.3 1.3 copy-done.6
  106.6 9.3 %shard_map.459.hidden.refs_1_ = bf16[2,1024,768]{2,1,0:T(8,128)(2,1)S(1)} custom-call(s32[8]{0:T(128)S(1)} %copy-done.43, bf16[256,768]{1,0:T(8,128)(2,1)S(1)} %get-tuple-element.86.refs_0_, bf16[256,768]{1,0:T(8,128)(2,1)S(1)} %get-tuple-element.87.refs_1_, bf16[256,768]{1,0:T(8,128)(2,1)S(1)} %collective-permute-done.17.refs_2_, ...), custom_call_target="tpu_custom_call" | custom-call | tf_op jit(solution)/shard_map/pallas_call | solution.py:371
  115.9 7.6 %shard_map.460 = (f32[512,768]{1,0:T(8,128)S(1)}, f32[512,768]{1,0:T(8,128)}) custom-call(s32[8]{0:T(128)S(1)} %copy-done.43, bf16[2,1024,768]{2,1,0:T(8,128)(2,1)S(1)} %shard_map.459.hidden.refs_1_, bf16[1,4,96,768]{3,2,1,0:T(8,128)(2,1)S(1)} %bitcast.77, ...), custom_call_target="tpu_custom_call" | custom-call | tf_op jit(solution)/shard_map/pallas_call | solution.py:402
  123.5 1.1 copy-done.20
  124.6 1.2 collective-permute-start.31
  125.8 2.5 %collective-permute-done.27.got = f32[512,768]{1,0:T(8,128)} collective-permute-done((f32[512,768]{1,0:T(8,128)}, f32[512,768]{1,0:T(8,128)}, u32[]{:S(2)}, u32[]{:S(2)}) %collective-permute-start.27) | collective-permute-done | bytes 1572896 | tf_op jit(solution)/shard_map/ppermute | solution.py:56
  128.4 1.4 copy-done.19
  129.8 1.4 copy-done.21
  131.2 3.8 %shard_map.461 = (bf16[512,768]{1,0:T(8,128)(2,1)}, bf16[128,768]{1,0:T(8,128)(2,1)S(1)}, f32[128,768]{1,0:T(8,128)S(1)}, f32[2,768]{1,0:T(2,128)S(1)}) custom-call(f32[512,768]{1,0:T(8,128)S(1)} %copy-done.19, f32[512,768]{1,0:T(8,128)S(1)} %copy-done.21, f32[512,768]{1,0:T(8,128)} %collective-permute-done.27.got, f32[4,768]{1,0:T(4,128)S(1)} %copy-done.42, ...), custom_call_target="tpu_custom_call" | custom-call | tf_op jit(solution)/shard_map/pallas_call | solution.py:459
  135.0 1.1 collective-permute-start.28
  136.7 5.2 %collective-permute-done.28.refs_1_ = bf16[128,768]{1,0:T(8,128)(2,1)S(1)} collective-permute-done((bf16[128,768]{1,0:T(8,128)(2,1)S(1)}, bf16[128,768]{1,0:T(8,128)(2,1)S(1)}, u32[]{:S(2)}, u32[]{:S(2)}) %collective-permute-start.28) | collective-permute-done | bytes 196640 | tf_op jit(solution)/shard_map/ppermute | solution.py:56
  142.0 1.4 collective-permute-done.30.refs_3_
  143.4 6.6 %shard_map.463 = (f32[2,128,768]{2,1,0:T(8,128)S(1)}, f32[2,128,768]{2,1,0:T(8,128)S(1)}, bf16[512,768]{1,0:T(8,128)(2,1)S(1)}, bf16[512,768]{1,0:T(8,128)(2,1)S...) custom-call(s32[8]{0:T(128)S(1)} %copy-done.44, ...), custom_call_target="tpu_custom_call" | custom-call | tf_op jit(solution)/shard_map/pallas_call | solution.py:506
  150.2 2.1 shard_map.464
  152.3 1.4 collective-permute-start.36
  153.7 1.4 shard_map.465
  155.3 1.1 collective-permute-start.35
  156.5 5.8 %collective-permute-done.35.got = bf16[128,768]{1,0:T(8,128)(2,1)S(1)} collective-permute-done((bf16[128,768]{1,0:T(8,128)(2,1)S(1)}, bf16[128,768]{1,0:T(8,128)(2,1)S(1)}, u32[]{:S(2)}, u32[]{:S(2)}) %collective-permute-start.35) | collective-permute-done | bytes 196640 | tf_op jit(solution)/shard_map/ppermute | solution.py:56
  162.3 11.1 %shard_map.466 = (f32[512,768]{1,0:T(8,128)S(1)}, bf16[512,2304]{1,0:T(8,128)(2,1)S(1)}, f32[2,768]{1,0:T(2,128)}, bf16[4,112,768]{2,1,0:T(8,128)(2,1)S(1)}, bf1...) custom-call(s32[8]{0:T(128)S(1)} %copy-done.44, ...), custom_call_target="tpu_custom_call" | custom-call | tf_op jit(solution)/shard_map/pallas_call | solution.py:780
  174.4 1.1 collective-permute-done.37.got
  178.7 1.1 collective-permute-start.43
  181.5 12.3 %collective-permute-done.42._.got = bf16[4,1,96,768]{3,2,1,0:T(8,128)(2,1)S(1)} collective-permute-done((bf16[4,1,96,768]{3,2,1,0:T(8,128)(2,1)S(1)}, bf16[4,1,96,768]{3,2,1,0:T(8,128)(2,1)S(1)}, u32[]{:S(2)}, u32[]{:S(2)}) %collective-permute-start.42) | collective-permute-done | bytes 589856 | tf_op jit(solution)/shard_map/ppermute | solution.py:56
  193.8 6.8 %collective-permute-done.44.corner_y = bf16[2,112,768]{2,1,0:T(8,128)(2,1)S(1)} collective-permute-done((bf16[2,112,768]{2,1,0:T(8,128)(2,1)S(1)}, bf16[2,112,768]{2,1,0:T(8,128)(2,1)S(1)}, u32[]{:S(2)}, u32[]{:S(2)}) %collective-permute-start.44) | collective-permute-done | bytes 344096 | tf_op jit(solution)/shard_map/ppermute | solution.py:56
  201.1 1.2 collective-permute-start.45
  202.2 1.3 collective-permute-start.46
  203.9 2.6 %collective-permute-start.50 = (bf16[2,96,768]{2,1,0:T(8,128)(2,1)S(1)}, bf16[2,96,768]{2,1,0:T(8,128)(2,1)S(1)}, u32[]{:S(2)}, u32[]{:S(2)}) collective-permute-start(bf16[2,96,768]{2,1,0:T(8,128)(2,1)S(1)} %bitcast.90), channel_id=1, source_target_pairs={{0,16},{4,20},{8,24},{12,28},{16,0},{20,4},{24,8},{28,12},{1,17},{... | collective-permute-start | bytes 884744 | tf_op jit(solution)/shard_map/ppermute | solution.py:56
  207.3 3.2 %shard_map.472._.refs_0_ = f32[512,768]{1,0:T(8,128)} custom-call(f32[512,768]{1,0:T(8,128)S(1)} %get-tuple-element.111.placed, bf16[512,2304]{1,0:T(8,128)(2,1)S(1)} %get-tuple-element.112.mixed_back, bf16[768,2304]{1,0:T(8,128)(2,1)S(1)} %copy-done.8, bf16[1,2,96,768]{3,2,1,0:T(8,128)(2,1)S(1)} %get-tuple-element.129._), custom_call_target="tpu_custom_call" | custom-call | tf_op jit(solution)/shard_map/pallas_call | solution.py:653
  210.4 6.7 %collective-permute-done.51.got = bf16[2,1,96,768]{3,2,1,0:T(8,128)(2,1)S(1)} collective-permute-done((bf16[2,1,96,768]{3,2,1,0:T(8,128)(2,1)S(1)}, bf16[2,1,96,768]{3,2,1,0:T(8,128)(2,1)S(1)}, u32[]{:S(2)}, u32[]{:S(2)}) %collective-permute-start.51) | collective-permute-done | bytes 294944 | tf_op jit(solution)/shard_map/ppermute | solution.py:56
  217.2 1.4 copy-done.2
  218.8 1.1 copy-done.3
  221.0 1.8 collective-permute-start.49
  223.6 1.8 collective-permute-start.47
  229.7 4.6 %collective-permute-done.52.refs_0_ = bf16[1,96,768]{2,1,0:T(8,128)(2,1)S(1)} collective-permute-done((bf16[1,96,768]{2,1,0:T(8,128)(2,1)S(1)}, bf16[1,96,768]{2,1,0:T(8,128)(2,1)S(1)}, u32[]{:S(2)}, u32[]{:S(2)}) %collective-permute-start.52) | collective-permute-done | bytes 147488 | tf_op jit(solution)/shard_map/ppermute | solution.py:56
  235.0 2.0 multiply_subtract_fusion.1
  237.1 4.1 %collective-permute-done.48 = bf16[112,768]{1,0:T(8,128)(2,1)S(1)} collective-permute-done((bf16[112,768]{1,0:T(8,128)(2,1)S(1)}, bf16[112,768]{1,0:T(8,128)(2,1)S(1)}, u32[]{:S(2)}, u32[]{:S(2)}) %collective-permute-start.48) | collective-permute-done | bytes 172064 | tf_op jit(solution)/shard_map/ppermute | solution.py:56
  242.1 1.2 multiply_subtract_fusion.3
  (275 shorter events, 41.0 us)
Async XLA Ops:
  4.0 10.9 %copy-start.73 = (s32[4,32]{1,0:T(4,128)S(1)}, s32[4,32]{1,0:T(4,128)}, u32[]{:S(2)}) copy-start(s32[4,32]{1,0:T(4,128)} %param.28) | copy-start | bytes 1540
  4.0 18.4 %copy-start.27 = (f32[96,768]{1,0:T(8,128)S(1)}, f32[96,768]{1,0:T(8,128)}, u32[]{:S(2)}) copy-start(f32[96,768]{1,0:T(8,128)} %first.1) | copy-start | bytes 884740
  4.0 18.3 %copy-start.29 = (f32[96,768]{1,0:T(8,128)S(1)}, f32[96,768]{1,0:T(8,128)}, u32[]{:S(2)}) copy-start(f32[96,768]{1,0:T(8,128)} %second.1) | copy-start | bytes 884740
  4.3 22.4 %copy-start.49 = (bf16[1,112,768]{2,1,0:T(8,128)(2,1)}, bf16[1,112,768]{2,1,0:T(8,128)(2,1)S(1)}, u32[]{:S(2)}) copy-start(bf16[1,112,768]{2,1,0:T(8,128)(2,1)S(1)} %pad_maximum_fusion.3.refs_0_) | copy-start | bytes 516100
  4.3 7.9 %collective-permute-start = (bf16[1,112,768]{2,1,0:T(8,128)(2,1)S(1)}, bf16[1,112,768]{2,1,0:T(8,128)(2,1)S(1)}, u32[]{:S(2)}, u32[]{:S(2)}) collective-permute-start(bf16[1,112,768]{2,1,0:T(8,128)(2,1)S(1)} %pad_maximum_fusion.3.refs_0_), channel_id=1, source_target_pairs={{0,8},{4,12},{8,0},{12,4},{16,24},{20,28},{24,16},{28,20},{1,9},{5... | collective-permute-start | bytes 516104 | tf_op jit(solution)/shard_map/ppermute | solution.py:56
  7.4 19.3 %collective-permute-start.5 = (bf16[1,112,768]{2,1,0:T(8,128)(2,1)S(1)}, bf16[1,112,768]{2,1,0:T(8,128)(2,1)S(1)}, u32[]{:S(2)}, u32[]{:S(2)}) collective-permute-start(bf16[1,112,768]{2,1,0:T(8,128)(2,1)S(1)} %pad_maximum_fusion.3.refs_0_), channel_id=1, source_target_pairs={{0,24},{4,28},{8,16},{12,20},{16,8},{20,12},{24,0},{28,4},{1,25},{... | collective-permute-start | bytes 516104 | tf_op jit(solution)/shard_map/ppermute | solution.py:56
  9.9 16.8 %collective-permute-start.4 = (bf16[1,112,768]{2,1,0:T(8,128)(2,1)S(1)}, bf16[1,112,768]{2,1,0:T(8,128)(2,1)S(1)}, u32[]{:S(2)}, u32[]{:S(2)}) collective-permute-start(bf16[1,112,768]{2,1,0:T(8,128)(2,1)S(1)} %pad_maximum_fusion.3.refs_0_), channel_id=1, source_target_pairs={{0,16},{4,20},{8,24},{12,28},{16,0},{20,4},{24,8},{28,12},{1,17},{... | collective-permute-start | bytes 516104 | tf_op jit(solution)/shard_map/ppermute | solution.py:56
  12.9 12.0 %copy-start.50 = (bf16[1,96,768]{2,1,0:T(8,128)(2,1)S(1)}, bf16[1,96,768]{2,1,0:T(8,128)(2,1)}, u32[]{:S(2)}) copy-start(bf16[1,96,768]{2,1,0:T(8,128)(2,1)} %shard_map.449) | copy-start | bytes 442372
  12.9 5.4 %collective-permute-start.1 = (bf16[1,96,768]{2,1,0:T(8,128)(2,1)}, bf16[1,96,768]{2,1,0:T(8,128)(2,1)S(1)}, u32[]{:S(2)}, u32[]{:S(2)}) collective-permute-start(bf16[1,96,768]{2,1,0:T(8,128)(2,1)} %shard_map.449), channel_id=1, source_target_pairs={{0,4},{4,0},{8,12},{12,8},{16,20},{20,16},{24,28},{28,24},{1,5},{5... | collective-permute-start | bytes 442376 | tf_op jit(solution)/shard_map/ppermute | solution.py:56
  15.0 9.8 %collective-permute-start.2 = (bf16[1,96,768]{2,1,0:T(8,128)(2,1)}, bf16[1,96,768]{2,1,0:T(8,128)(2,1)S(1)}, u32[]{:S(2)}, u32[]{:S(2)}) collective-permute-start(bf16[1,96,768]{2,1,0:T(8,128)(2,1)} %shard_map.449), channel_id=1, source_target_pairs={{0,2},{1,3},{2,0},{3,1},{4,6},{5,7},{6,4},{7,5},{8,10},{9,11},{10,... | collective-permute-start | bytes 442376 | tf_op jit(solution)/shard_map/ppermute | solution.py:56
  18.2 6.6 %collective-permute-start.3 = (bf16[1,96,768]{2,1,0:T(8,128)(2,1)S(1)}, bf16[1,96,768]{2,1,0:T(8,128)(2,1)S(1)}, u32[]{:S(2)}, u32[]{:S(2)}) collective-permute-start(bf16[1,96,768]{2,1,0:T(8,128)(2,1)S(1)} %collective-permute-done.1.refs_1_), channel_id=1, source_target_pairs={{0,2},{1,3},{2,0},{3,1},{4,6},{5,7},{6,4},{7,5},{8,10},{9,11},{10,... | collective-permute-start | bytes 442376 | tf_op jit(solution)/shard_map/ppermute | solution.py:56
  27.9 20.7 %copy-start.11 = (bf16[4,1,112,768]{3,2,1,0:T(8,128)(2,1)}, bf16[4,1,112,768]{3,2,1,0:T(8,128)(2,1)S(1)}, u32[]{:S(2)}) copy-start(bf16[4,1,112,768]{3,2,1,0:T(8,128)(2,1)S(1)} %pad_maximum_fusion.1.refs_0_) | copy-start | bytes 2064388
  27.9 16.6 %collective-permute-start.6 = (bf16[4,1,112,768]{3,2,1,0:T(8,128)(2,1)S(1)}, bf16[4,1,112,768]{3,2,1,0:T(8,128)(2,1)}, u32[]{:S(2)}, u32[]{:S(2)}) collective-permute-start(bf16[4,1,112,768]{3,2,1,0:T(8,128)(2,1)S(1)} %pad_maximum_fusion.1.refs_0_), channel_id=1, source_target_pairs={{0,4},{4,0},{8,12},{12,8},{16,20},{20,16},{24,28},{28,24},{1,5},{5... | collective-permute-start | bytes 2064392 | tf_op jit(solution)/shard_map/ppermute | solution.py:56
  29.5 15.0 %collective-permute-start.7 = (bf16[4,1,112,768]{3,2,1,0:T(8,128)(2,1)S(1)}, bf16[4,1,112,768]{3,2,1,0:T(8,128)(2,1)}, u32[]{:S(2)}, u32[]{:S(2)}) collective-permute-start(bf16[4,1,112,768]{3,2,1,0:T(8,128)(2,1)S(1)} %pad_maximum_fusion.1.refs_0_), channel_id=1, source_target_pairs={{0,2},{1,3},{2,0},{3,1},{4,6},{5,7},{6,4},{7,5},{8,10},{9,11},{10,... | collective-permute-start | bytes 2064392 | tf_op jit(solution)/shard_map/ppermute | solution.py:56
  30.0 11.3 %copy-start.56 = (bf16[512,768]{1,0:T(8,128)(2,1)S(1)}, bf16[512,768]{1,0:T(8,128)(2,1)}, u32[]{:S(2)}) copy-start(bf16[512,768]{1,0:T(8,128)(2,1)} %param.26) | copy-start | bytes 2359300
  30.0 14.3 %collective-permute-start.8 = (bf16[2,96,768]{2,1,0:T(8,128)(2,1)}, bf16[2,96,768]{2,1,0:T(8,128)(2,1)S(1)}, u32[]{:S(2)}, u32[]{:S(2)}) collective-permute-start(bf16[2,96,768]{2,1,0:T(8,128)(2,1)} %shard_map.453.refs_0_), channel_id=1, source_target_pairs={{0,16},{4,20},{8,24},{12,28},{16,0},{20,4},{24,8},{28,12},{1,17},{... | collective-permute-start | bytes 884744 | tf_op jit(solution)/shard_map/ppermute | solution.py:56
  33.6 10.9 %collective-permute-start.9 = (bf16[2,96,768]{2,1,0:T(8,128)(2,1)}, bf16[2,96,768]{2,1,0:T(8,128)(2,1)S(1)}, u32[]{:S(2)}, u32[]{:S(2)}) collective-permute-start(bf16[2,96,768]{2,1,0:T(8,128)(2,1)} %shard_map.453.refs_0_), channel_id=1, source_target_pairs={{0,8},{4,12},{8,0},{12,4},{16,24},{20,28},{24,16},{28,20},{1,9},{5... | collective-permute-start | bytes 884744 | tf_op jit(solution)/shard_map/ppermute | solution.py:56
  44.3 11.4 %copy-start.13 = (bf16[2,96,768]{2,1,0:T(8,128)(2,1)}, bf16[2,96,768]{2,1,0:T(8,128)(2,1)S(1)}, u32[]{:S(2)}) copy-start(bf16[2,96,768]{2,1,0:T(8,128)(2,1)S(1)} %collective-permute-done.8.refs_0_.refs_1_) | copy-start | bytes 884740
  44.5 11.3 %copy-start.14 = (bf16[2,96,768]{2,1,0:T(8,128)(2,1)}, bf16[2,96,768]{2,1,0:T(8,128)(2,1)S(1)}, u32[]{:S(2)}) copy-start(bf16[2,96,768]{2,1,0:T(8,128)(2,1)S(1)} %collective-permute-done.9.refs_1_.refs_2_) | copy-start | bytes 884740
  45.7 9.3 %collective-permute-start.10 = (bf16[2,1,112,768]{3,2,1,0:T(8,128)(2,1)S(1)}, bf16[2,1,112,768]{3,2,1,0:T(8,128)(2,1)}, u32[]{:S(2)}, u32[]{:S(2)}) collective-permute-start(bf16[2,1,112,768]{3,2,1,0:T(8,128)(2,1)S(1)} %get-tuple-element.83), channel_id=1, source_target_pairs={{0,2},{1,3},{2,0},{3,1},{4,6},{5,7},{6,4},{7,5},{8,10},{9,11},{10,... | collective-permute-start | bytes 1032200 | tf_op jit(solution)/shard_map/ppermute | solution.py:56
  46.6 8.4 %collective-permute-start.11 = (bf16[2,1,112,768]{3,2,1,0:T(8,128)(2,1)S(1)}, bf16[2,1,112,768]{3,2,1,0:T(8,128)(2,1)S(1)}, u32[]{:S(2)}, u32[]{:S(2)}) collective-permute-start(bf16[2,1,112,768]{3,2,1,0:T(8,128)(2,1)S(1)} %get-tuple-element.84), channel_id=1, source_target_pairs={{0,4},{4,0},{8,12},{12,8},{16,20},{20,16},{24,28},{28,24},{1,5},{5... | collective-permute-start | bytes 1032200 | tf_op jit(solution)/shard_map/ppermute | solution.py:56
  47.1 8.6 %collective-permute-start.19 = (bf16[2,96,768]{2,1,0:T(8,128)(2,1)S(1)}, bf16[2,96,768]{2,1,0:T(8,128)(2,1)S(1)}, u32[]{:S(2)}, u32[]{:S(2)}) collective-permute-start(bf16[2,96,768]{2,1,0:T(8,128)(2,1)S(1)} %collective-permute-done.8.refs_0_.refs_1_), channel_id=1, source_target_pairs={{0,8},{4,12},{8,0},{12,4},{16,24},{20,28},{24,16},{28,20},{1,9},{5... | collective-permute-start | bytes 884744 | tf_op jit(solution)/shard_map/ppermute | solution.py:56
  48.5 11.8 %collective-permute-start.12 = (bf16[4,1,112,768]{3,2,1,0:T(8,128)(2,1)S(1)}, bf16[4,1,112,768]{3,2,1,0:T(8,128)(2,1)}, u32[]{:S(2)}, u32[]{:S(2)}) collective-permute-start(bf16[4,1,112,768]{3,2,1,0:T(8,128)(2,1)S(1)} %pad_maximum_fusion.1.refs_0_), channel_id=1, source_target_pairs={{0,1},{1,0},{2,3},{3,2},{4,5},{5,4},{6,7},{7,6},{8,9},{9,8},{10,11... | collective-permute-start | bytes 2064392 | tf_op jit(solution)/shard_map/ppermute | solution.py:56
  48.5 11.8 %collective-permute-start.13 = (bf16[4,1,112,768]{3,2,1,0:T(8,128)(2,1)}, bf16[4,1,112,768]{3,2,1,0:T(8,128)(2,1)}, u32[]{:S(2)}, u32[]{:S(2)}) collective-permute-start(bf16[4,1,112,768]{3,2,1,0:T(8,128)(2,1)} %collective-permute-done.6.from_y.refs_1_), channel_id=1, source_target_pairs={{0,1},{1,0},{2,3},{3,2},{4,5},{5,4},{6,7},{7,6},{8,9},{9,8},{10,11... | collective-permute-start | bytes 2064392 | tf_op jit(solution)/shard_map/ppermute | solution.py:56
  55.0 5.4 %collective-permute-start.14 = (bf16[4,1,112,768]{3,2,1,0:T(8,128)(2,1)}, bf16[4,1,112,768]{3,2,1,0:T(8,128)(2,1)}, u32[]{:S(2)}, u32[]{:S(2)}) collective-permute-start(bf16[4,1,112,768]{3,2,1,0:T(8,128)(2,1)} %collective-permute-done.7.from_x.refs_2_), channel_id=1, source_target_pairs={{0,1},{1,0},{2,3},{3,2},{4,5},{5,4},{6,7},{7,6},{8,9},{9,8},{10,11... | collective-permute-start | bytes 2064392 | tf_op jit(solution)/shard_map/ppermute | solution.py:56
  58.0 30.1 %collective-permute-start.20 = (bf16[4,2,96,768]{3,2,1,0:T(8,128)(2,1)}, bf16[4,2,96,768]{3,2,1,0:T(8,128)(2,1)}, u32[]{:S(2)}, u32[]{:S(2)}) collective-permute-start(bf16[4,2,96,768]{3,2,1,0:T(8,128)(2,1)} %pad_maximum_fusion.refs_4_.refs_8_), channel_id=1, source_target_pairs={{0,4},{4,0},{8,12},{12,8},{16,20},{20,16},{24,28},{28,24},{1,5},{5... | collective-permute-start | bytes 3538952 | tf_op jit(solution)/shard_map/ppermute | solution.py:56
  58.7 29.5 %collective-permute-start.21 = (bf16[4,2,96,768]{3,2,1,0:T(8,128)(2,1)}, bf16[4,2,96,768]{3,2,1,0:T(8,128)(2,1)S(1)}, u32[]{:S(2)}, u32[]{:S(2)}) collective-permute-start(bf16[4,2,96,768]{3,2,1,0:T(8,128)(2,1)} %pad_maximum_fusion.refs_4_.refs_8_), channel_id=1, source_target_pairs={{0,2},{1,3},{2,0},{3,1},{4,6},{5,7},{6,4},{7,5},{8,10},{9,11},{10,... | collective-permute-start | bytes 3538952 | tf_op jit(solution)/shard_map/ppermute | solution.py:56
  60.3 2.6 %collective-permute-start.15 = (bf16[2,1,112,768]{3,2,1,0:T(8,128)(2,1)}, bf16[2,1,112,768]{3,2,1,0:T(8,128)(2,1)}, u32[]{:S(2)}, u32[]{:S(2)}) collective-permute-start(bf16[2,1,112,768]{3,2,1,0:T(8,128)(2,1)} %collective-permute-done.10.refs_3_.refs_1_), channel_id=1, source_target_pairs={{0,1},{1,0},{2,3},{3,2},{4,5},{5,4},{6,7},{7,6},{8,9},{9,8},{10,11... | collective-permute-start | bytes 1032200 | tf_op jit(solution)/shard_map/ppermute | solution.py:56
  60.3 27.8 %collective-permute-start.22 = (bf16[1,4,96,768]{3,2,1,0:T(8,128)(2,1)}, bf16[1,4,96,768]{3,2,1,0:T(8,128)(2,1)S(1)}, u32[]{:S(2)}, u32[]{:S(2)}) collective-permute-start(bf16[1,4,96,768]{3,2,1,0:T(8,128)(2,1)} %bitcast.75), channel_id=1, source_target_pairs={{0,8},{4,12},{8,0},{12,4},{16,24},{20,28},{24,16},{28,20},{1,9},{5... | collective-permute-start | bytes 1769480 | tf_op jit(solution)/shard_map/ppermute | solution.py:56
  60.4 31.6 %collective-permute-start.25 = (bf16[1,4,96,768]{3,2,1,0:T(8,128)(2,1)}, bf16[1,4,96,768]{3,2,1,0:T(8,128)(2,1)S(1)}, u32[]{:S(2)}, u32[]{:S(2)}) collective-permute-start(bf16[1,4,96,768]{3,2,1,0:T(8,128)(2,1)} %bitcast.76), channel_id=1, source_target_pairs={{0,16},{4,20},{8,24},{12,28},{16,0},{20,4},{24,8},{28,12},{1,17},{... | collective-permute-start | bytes 1769480 | tf_op jit(solution)/shard_map/ppermute | solution.py:56
  62.9 1.7 collective-permute-start.16
  89.7 14.9 %collective-permute-start.23 = (bf16[2,2,96,768]{3,2,1,0:T(8,128)(2,1)S(1)}, bf16[2,2,96,768]{3,2,1,0:T(8,128)(2,1)S(1)}, u32[]{:S(2)}, u32[]{:S(2)}) collective-permute-start(bf16[2,2,96,768]{3,2,1,0:T(8,128)(2,1)S(1)} %get-tuple-element.88), channel_id=1, source_target_pairs={{0,2},{1,3},{2,0},{3,1},{4,6},{5,7},{6,4},{7,5},{8,10},{9,11},{10,... | collective-permute-start | bytes 1769480 | tf_op jit(solution)/shard_map/ppermute | solution.py:56
  90.7 14.6 %collective-permute-start.24 = (bf16[2,2,96,768]{3,2,1,0:T(8,128)(2,1)S(1)}, bf16[2,2,96,768]{3,2,1,0:T(8,128)(2,1)S(1)}, u32[]{:S(2)}, u32[]{:S(2)}) collective-permute-start(bf16[2,2,96,768]{3,2,1,0:T(8,128)(2,1)S(1)} %get-tuple-element.89), channel_id=1, source_target_pairs={{0,4},{4,0},{8,12},{12,8},{16,20},{20,16},{24,28},{28,24},{1,5},{5... | collective-permute-start | bytes 1769480 | tf_op jit(solution)/shard_map/ppermute | solution.py:56
  92.0 23.8 %collective-permute-start.26 = (bf16[1,4,96,768]{3,2,1,0:T(8,128)(2,1)S(1)}, bf16[1,4,96,768]{3,2,1,0:T(8,128)(2,1)S(1)}, u32[]{:S(2)}, u32[]{:S(2)}) collective-permute-start(bf16[1,4,96,768]{3,2,1,0:T(8,128)(2,1)S(1)} %collective-permute-done.25.refs_9_.refs_1_.refs_5_.refs_13_.refs_11_.refs_15_), channel_id=1, source_target_pairs={{0,8},{4,12},{8,0},{12,4},{16,24},{20,28},{24,16},{28,20},{1,9},{5... | collective-permute-start | bytes 1769480 | tf_op jit(solution)/shard_map/ppermute | solution.py:56
  92.0 1.7 collective-permute-start.17
  92.0 23.8 %copy-start = (bf16[4,96,768]{2,1,0:T(8,128)(2,1)S(1)}, bf16[4,96,768]{2,1,0:T(8,128)(2,1)}, u32[]{:S(2)}) copy-start(bf16[4,96,768]{2,1,0:T(8,128)(2,1)} %shard_map.457) | copy-start | bytes 1769476
  92.0 2.3 collective-permute-start.18
  124.6 3.8 %collective-permute-start.27 = (f32[512,768]{1,0:T(8,128)}, f32[512,768]{1,0:T(8,128)}, u32[]{:S(2)}, u32[]{:S(2)}) collective-permute-start(f32[512,768]{1,0:T(8,128)} %get-tuple-element.91), channel_id=1, source_target_pairs={{0,1},{1,0},{2,3},{3,2},{4,5},{5,4},{6,7},{7,6},{8,9},{9,8},{10,11... | collective-permute-start | bytes 4718600 | tf_op jit(solution)/shard_map/ppermute | solution.py:56
  124.6 11.5 %collective-permute-start.31 = (bf16[128,768]{1,0:T(8,128)(2,1)}, bf16[128,768]{1,0:T(8,128)(2,1)S(1)}, u32[]{:S(2)}, u32[]{:S(2)}) collective-permute-start(bf16[128,768]{1,0:T(8,128)(2,1)} %shard_map.462.refs_4_), channel_id=1, source_target_pairs={{0,2},{1,3},{2,0},{3,1},{4,6},{5,7},{6,4},{7,5},{8,10},{9,11},{10,... | collective-permute-start | bytes 589832 | tf_op jit(solution)/shard_map/ppermute | solution.py:56
  131.2 12.2 %copy-start.44 = (s32[8]{0:T(128)S(1)}, s32[8]{0:T(128)}, u32[]{:S(2)}) copy-start(s32[8]{0:T(128)} %broadcast_multiply_fusion.refs_3_.rows.refs_16_) | copy-start | bytes 100
  135.0 6.9 %collective-permute-start.28 = (bf16[128,768]{1,0:T(8,128)(2,1)S(1)}, bf16[128,768]{1,0:T(8,128)(2,1)S(1)}, u32[]{:S(2)}, u32[]{:S(2)}) collective-permute-start(bf16[128,768]{1,0:T(8,128)(2,1)S(1)} %get-tuple-element.95.refs_0_), channel_id=1, source_target_pairs={{0,2},{1,3},{2,0},{3,1},{4,6},{5,7},{6,4},{7,5},{8,10},{9,11},{10,... | collective-permute-start | bytes 589832 | tf_op jit(solution)/shard_map/ppermute | solution.py:56
  136.2 5.8 %collective-permute-start.32 = (bf16[128,768]{1,0:T(8,128)(2,1)S(1)}, bf16[128,768]{1,0:T(8,128)(2,1)S(1)}, u32[]{:S(2)}, u32[]{:S(2)}) collective-permute-start(bf16[128,768]{1,0:T(8,128)(2,1)S(1)} %copy-done.34), channel_id=1, source_target_pairs={{0,1},{1,0},{2,3},{3,2},{4,5},{5,4},{6,7},{7,6},{8,9},{9,8},{10,11... | collective-permute-start | bytes 589832 | tf_op jit(solution)/shard_map/ppermute | solution.py:56
  136.2 5.8 %collective-permute-start.33 = (bf16[128,768]{1,0:T(8,128)(2,1)S(1)}, bf16[128,768]{1,0:T(8,128)(2,1)S(1)}, u32[]{:S(2)}, u32[]{:S(2)}) collective-permute-start(bf16[128,768]{1,0:T(8,128)(2,1)S(1)} %collective-permute-done.31.refs_5_), channel_id=1, source_target_pairs={{0,1},{1,0},{2,3},{3,2},{4,5},{5,4},{6,7},{7,6},{8,9},{9,8},{10,11... | collective-permute-start | bytes 589832 | tf_op jit(solution)/shard_map/ppermute | solution.py:56
  136.7 5.3 %collective-permute-start.29 = (bf16[128,768]{1,0:T(8,128)(2,1)S(1)}, bf16[128,768]{1,0:T(8,128)(2,1)S(1)}, u32[]{:S(2)}, u32[]{:S(2)}) collective-permute-start(bf16[128,768]{1,0:T(8,128)(2,1)S(1)} %get-tuple-element.95.refs_0_), channel_id=1, source_target_pairs={{0,1},{1,0},{2,3},{3,2},{4,5},{5,4},{6,7},{7,6},{8,9},{9,8},{10,11... | collective-permute-start | bytes 589832 | tf_op jit(solution)/shard_map/ppermute | solution.py:56
  142.0 1.4 collective-permute-start.30
  150.0 5.2 %collective-permute-start.34 = (f32[2,128,768]{2,1,0:T(8,128)S(1)}, f32[2,128,768]{2,1,0:T(8,128)S(1)}, u32[]{:S(2)}, u32[]{:S(2)}) collective-permute-start(f32[2,128,768]{2,1,0:T(8,128)S(1)} %get-tuple-element.98), channel_id=1, source_target_pairs={{0,1},{1,0},{2,3},{3,2},{4,5},{5,4},{6,7},{7,6},{8,9},{9,8},{10,11... | collective-permute-start | bytes 2359304 | tf_op jit(solution)/shard_map/ppermute | solution.py:56
  152.3 28.9 %collective-permute-start.36 = (bf16[4,2,96,768]{3,2,1,0:T(8,128)(2,1)S(1)}, bf16[4,2,96,768]{3,2,1,0:T(8,128)(2,1)S(1)}, u32[]{:S(2)}, u32[]{:S(2)}) collective-permute-start(bf16[4,2,96,768]{3,2,1,0:T(8,128)(2,1)S(1)} %get-tuple-element.114), channel_id=1, source_target_pairs={{0,4},{4,0},{8,12},{12,8},{16,20},{20,16},{24,28},{28,24},{1,5},{5... | collective-permute-start | bytes 3538952 | tf_op jit(solution)/shard_map/ppermute | solution.py:56
  155.3 7.0 %collective-permute-start.35 = (bf16[128,768]{1,0:T(8,128)(2,1)S(1)}, bf16[128,768]{1,0:T(8,128)(2,1)S(1)}, u32[]{:S(2)}, u32[]{:S(2)}) collective-permute-start(bf16[128,768]{1,0:T(8,128)(2,1)S(1)} %fusion.6), channel_id=1, source_target_pairs={{0,2},{1,3},{2,0},{3,1},{4,6},{5,7},{6,4},{7,5},{8,10},{9,11},{10,... | collective-permute-start | bytes 589832 | tf_op jit(solution)/shard_map/ppermute | solution.py:56
  173.4 2.1 collective-permute-start.37
  173.4 3.1 %collective-permute-start.38 = (bf16[4,112,768]{2,1,0:T(8,128)(2,1)S(1)}, bf16[4,112,768]{2,1,0:T(8,128)(2,1)S(1)}, u32[]{:S(2)}, u32[]{:S(2)}) collective-permute-start(bf16[4,112,768]{2,1,0:T(8,128)(2,1)S(1)} %get-tuple-element.117), channel_id=1, source_target_pairs={{0,1},{1,0},{2,3},{3,2},{4,5},{5,4},{6,7},{7,6},{8,9},{9,8},{10,11... | collective-permute-start | bytes 2064392 | tf_op jit(solution)/shard_map/ppermute | solution.py:56
  173.9 3.6 %collective-permute-start.39 = (bf16[4,112,768]{2,1,0:T(8,128)(2,1)S(1)}, bf16[4,112,768]{2,1,0:T(8,128)(2,1)S(1)}, u32[]{:S(2)}, u32[]{:S(2)}) collective-permute-start(bf16[4,112,768]{2,1,0:T(8,128)(2,1)S(1)} %get-tuple-element.118), channel_id=1, source_target_pairs={{0,1},{1,0},{2,3},{3,2},{4,5},{5,4},{6,7},{7,6},{8,9},{9,8},{10,11... | collective-permute-start | bytes 2064392 | tf_op jit(solution)/shard_map/ppermute | solution.py:56
  173.9 4.6 %collective-permute-start.40 = (bf16[4,112,768]{2,1,0:T(8,128)(2,1)S(1)}, bf16[4,112,768]{2,1,0:T(8,128)(2,1)S(1)}, u32[]{:S(2)}, u32[]{:S(2)}) collective-permute-start(bf16[4,112,768]{2,1,0:T(8,128)(2,1)S(1)} %get-tuple-element.119), channel_id=1, source_target_pairs={{0,1},{1,0},{2,3},{3,2},{4,5},{5,4},{6,7},{7,6},{8,9},{9,8},{10,11... | collective-permute-start | bytes 2064392 | tf_op jit(solution)/shard_map/ppermute | solution.py:56
  175.5 18.3 %collective-permute-start.42 = (bf16[4,1,96,768]{3,2,1,0:T(8,128)(2,1)S(1)}, bf16[4,1,96,768]{3,2,1,0:T(8,128)(2,1)S(1)}, u32[]{:S(2)}, u32[]{:S(2)}) collective-permute-start(bf16[4,1,96,768]{3,2,1,0:T(8,128)(2,1)S(1)} %get-tuple-element.110._), channel_id=1, source_target_pairs={{0,4},{4,0},{8,12},{12,8},{16,20},{20,16},{24,28},{28,24},{1,5},{5... | collective-permute-start | bytes 1769480 | tf_op jit(solution)/shard_map/ppermute | solution.py:56
  178.7 15.2 %collective-permute-start.43 = (bf16[2,112,768]{2,1,0:T(8,128)(2,1)S(1)}, bf16[2,112,768]{2,1,0:T(8,128)(2,1)S(1)}, u32[]{:S(2)}, u32[]{:S(2)}) collective-permute-start(bf16[2,112,768]{2,1,0:T(8,128)(2,1)S(1)} %get-tuple-element.120.refs_0_), channel_id=1, source_target_pairs={{0,2},{1,3},{2,0},{3,1},{4,6},{5,7},{6,4},{7,5},{8,10},{9,11},{10,... | collective-permute-start | bytes 1032200 | tf_op jit(solution)/shard_map/ppermute | solution.py:56
  179.8 20.9 %collective-permute-start.44 = (bf16[2,112,768]{2,1,0:T(8,128)(2,1)S(1)}, bf16[2,112,768]{2,1,0:T(8,128)(2,1)S(1)}, u32[]{:S(2)}, u32[]{:S(2)}) collective-permute-start(bf16[2,112,768]{2,1,0:T(8,128)(2,1)S(1)} %get-tuple-element.126), channel_id=1, source_target_pairs={{0,4},{4,0},{8,12},{12,8},{16,20},{20,16},{24,28},{28,24},{1,5},{5... | collective-permute-start | bytes 1032200 | tf_op jit(solution)/shard_map/ppermute | solution.py:56
  181.5 22.3 %collective-permute-start.41 = (bf16[2,2,96,768]{3,2,1,0:T(8,128)(2,1)S(1)}, bf16[2,2,96,768]{3,2,1,0:T(8,128)(2,1)S(1)}, u32[]{:S(2)}, u32[]{:S(2)}) collective-permute-start(bf16[2,2,96,768]{3,2,1,0:T(8,128)(2,1)S(1)} %get-tuple-element.122), channel_id=1, source_target_pairs={{0,8},{4,12},{8,0},{12,4},{16,24},{20,28},{24,16},{28,20},{1,9},{5... | collective-permute-start | bytes 1769480 | tf_op jit(solution)/shard_map/ppermute | solution.py:56
  201.1 17.7 %collective-permute-start.45 = (bf16[4,112,768]{2,1,0:T(8,128)(2,1)S(1)}, bf16[4,112,768]{2,1,0:T(8,128)(2,1)S(1)}, u32[]{:S(2)}, u32[]{:S(2)}) collective-permute-start(bf16[4,112,768]{2,1,0:T(8,128)(2,1)S(1)} %get-tuple-element.127.refs_0_), channel_id=1, source_target_pairs={{0,2},{1,3},{2,0},{3,1},{4,6},{5,7},{6,4},{7,5},{8,10},{9,11},{10,... | collective-permute-start | bytes 2064392 | tf_op jit(solution)/shard_map/ppermute | solution.py:56
  202.2 16.6 %collective-permute-start.46 = (bf16[4,112,768]{2,1,0:T(8,128)(2,1)S(1)}, bf16[4,112,768]{2,1,0:T(8,128)(2,1)S(1)}, u32[]{:S(2)}, u32[]{:S(2)}) collective-permute-start(bf16[4,112,768]{2,1,0:T(8,128)(2,1)S(1)} %get-tuple-element.131), channel_id=1, source_target_pairs={{0,4},{4,0},{8,12},{12,8},{16,20},{20,16},{24,28},{28,24},{1,5},{5... | collective-permute-start | bytes 2064392 | tf_op jit(solution)/shard_map/ppermute | solution.py:56
  203.6 13.5 %collective-permute-start.51 = (bf16[2,1,96,768]{3,2,1,0:T(8,128)(2,1)S(1)}, bf16[2,1,96,768]{3,2,1,0:T(8,128)(2,1)S(1)}, u32[]{:S(2)}, u32[]{:S(2)}) collective-permute-start(bf16[2,1,96,768]{3,2,1,0:T(8,128)(2,1)S(1)} %get-tuple-element.128.refs_0_), channel_id=1, source_target_pairs={{0,8},{4,12},{8,0},{12,4},{16,24},{20,28},{24,16},{28,20},{1,9},{5... | collective-permute-start | bytes 884744 | tf_op jit(solution)/shard_map/ppermute | solution.py:56
  203.9 21.6 %collective-permute-start.50 = (bf16[2,96,768]{2,1,0:T(8,128)(2,1)S(1)}, bf16[2,96,768]{2,1,0:T(8,128)(2,1)S(1)}, u32[]{:S(2)}, u32[]{:S(2)}) collective-permute-start(bf16[2,96,768]{2,1,0:T(8,128)(2,1)S(1)} %bitcast.90), channel_id=1, source_target_pairs={{0,16},{4,20},{8,24},{12,28},{16,0},{20,4},{24,8},{28,12},{1,17},{... | collective-permute-start | bytes 884744 | tf_op jit(solution)/shard_map/ppermute | solution.py:56
  218.6 15.7 %collective-permute-start.52 = (bf16[1,96,768]{2,1,0:T(8,128)(2,1)S(1)}, bf16[1,96,768]{2,1,0:T(8,128)(2,1)S(1)}, u32[]{:S(2)}, u32[]{:S(2)}) collective-permute-start(bf16[1,96,768]{2,1,0:T(8,128)(2,1)S(1)} %bitcast.91), channel_id=1, source_target_pairs={{0,16},{4,20},{8,24},{12,28},{16,0},{20,4},{24,8},{28,12},{1,17},{... | collective-permute-start | bytes 442376 | tf_op jit(solution)/shard_map/ppermute | solution.py:56
  221.0 16.1 %collective-permute-start.49 = (bf16[112,768]{1,0:T(8,128)(2,1)S(1)}, bf16[112,768]{1,0:T(8,128)(2,1)S(1)}, u32[]{:S(2)}, u32[]{:S(2)}) collective-permute-start(bf16[112,768]{1,0:T(8,128)(2,1)S(1)} %get-tuple-element.135), channel_id=1, source_target_pairs={{0,24},{4,28},{8,16},{12,20},{16,8},{20,12},{24,0},{28,4},{1,25},{... | collective-permute-start | bytes 516104 | tf_op jit(solution)/shard_map/ppermute | solution.py:56
  222.8 18.4 %collective-permute-start.48 = (bf16[112,768]{1,0:T(8,128)(2,1)S(1)}, bf16[112,768]{1,0:T(8,128)(2,1)S(1)}, u32[]{:S(2)}, u32[]{:S(2)}) collective-permute-start(bf16[112,768]{1,0:T(8,128)(2,1)S(1)} %get-tuple-element.134), channel_id=1, source_target_pairs={{0,16},{4,20},{8,24},{12,28},{16,0},{20,4},{24,8},{28,12},{1,17},{... | collective-permute-start | bytes 516104 | tf_op jit(solution)/shard_map/ppermute | solution.py:56
  223.6 17.7 %collective-permute-start.47 = (bf16[112,768]{1,0:T(8,128)(2,1)S(1)}, bf16[112,768]{1,0:T(8,128)(2,1)S(1)}, u32[]{:S(2)}, u32[]{:S(2)}) collective-permute-start(bf16[112,768]{1,0:T(8,128)(2,1)S(1)} %get-tuple-element.133), channel_id=1, source_target_pairs={{0,8},{4,12},{8,0},{12,4},{16,24},{20,28},{24,16},{28,20},{1,9},{5... | collective-permute-start | bytes 516104 | tf_op jit(solution)/shard_map/ppermute | solution.py:56
  (69 other events, 251.0 us)
